TPU v7x, 128 devices: a whole 4x4x4 slice. The times are simulated.
128 devices in a mesh: band: 16 (over x_lo, y, core), space: 8 (over z, x_hi).
Axes of the slice: x: 4 (x_hi: 2, x_lo: 2; x = x_hi * 2 + x_lo), y: 4, z: 4, core: 2. Of those that a mesh axis runs over, the one named last changes fastest.
Arguments:
- orbitals: bfloat16 [16, 192, 192, 192], P('band', 'space'), may hold values from -4 to 4
- occupations: float32 [16], P('band'), may hold values from 0.25 to 1
- shifts: float32 [16], P('band'), may hold values from 0.25 to 2
- perturbations: float32 [1, 192, 192, 192], P(None, 'space'), may hold values from -3 to 3
- local_potential: float32 [192, 192, 192], P('space'), may hold values from 0 to 1
Outputs:
- response_potential: float32 [1, 192, 192, 192], P(None, 'space', 'band')
All inputs are finite; a program needn't handle non-finite values.
Results may differ from a plain program's by a relative error of at most 0.0003.
Values sent between devices are 32-bit elements; how exact they have to be, the bound alone decides.
A program may use at most 256 MiB of HBM per device.

v0:
```python
import math

import jax
import jax.numpy as jnp
from jax import lax
from jax.sharding import PartitionSpec as P

APPLY = 2


COEFFS = (-205.0 / 72.0, 8.0 / 5.0, -1.0 / 5.0, 8.0 / 315.0, -1.0 / 560.0)


def padded_2(cells, sides, width):
    for axis, dim in sides:
        count = lax.axis_size(axis)
        head = lax.slice_in_dim(cells, 0, width, axis=dim)
        tail = lax.slice_in_dim(cells, cells.shape[dim] - width, cells.shape[dim], axis=dim)
        cells = jnp.concatenate(
            [
                lax.ppermute(tail, axis, [(i, (i + 1) % count) for i in range(count)]),
                cells,
                lax.ppermute(head, axis, [((i + 1) % count, i) for i in range(count)]),
            ],
            axis=dim,
        )
    return cells


def cas_table(count):
    index = jnp.arange(count, dtype=jnp.int32)
    product = index[:, None] * index[None, :] % count
    angles = product.astype(jnp.float32) * (2.0 * math.pi / count)
    return jnp.cos(angles) + jnp.sin(angles)


def folded(values, count):
    return jnp.minimum(values, count - values).astype(jnp.float32)


def apply_operator(direction, potential_plus, count_x, grid):
    padded = padded_2(direction, (("space", 2),), 4)
    plane = direction.shape[3]
    zpos = jnp.arange(plane, dtype=jnp.int32) % grid
    total = 3.0 * COEFFS[0] * direction
    for offset in range(1, 5):
        upper = padded[:, :, 4 + offset : 4 + offset + count_x]
        lower = padded[:, :, 4 - offset : 4 - offset + count_x]
        total = total + COEFFS[offset] * (upper + lower)
        ys = jnp.roll(direction, offset * grid, 3) + jnp.roll(direction, -offset * grid, 3)
        total = total + COEFFS[offset] * ys
        z_low = jnp.where(
            zpos >= offset, jnp.roll(direction, offset, 3), jnp.roll(direction, offset - grid, 3)
        )
        z_high = jnp.where(
            zpos + offset < grid,
            jnp.roll(direction, -offset, 3),
            jnp.roll(direction, grid - offset, 3),
        )
        total = total + COEFFS[offset] * (z_low + z_high)
    return -0.5 * total + potential_plus * direction


def on_device(orbitals, occupations, shifts, perturbations, local_potential):
    highest = lax.Precision.HIGHEST
    orb_count = orbitals.shape[0]
    count_x = orbitals.shape[1]
    grid = orbitals.shape[2]
    pert_count = perturbations.shape[0]
    plane = grid * grid
    n_band = lax.axis_size("band")
    n_space = lax.axis_size("space")
    total_orbitals = orb_count * n_band
    wave = orbitals.reshape(orb_count, count_x, plane).astype(jnp.float32)[:, None]
    flat_pert = perturbations.reshape(pert_count, count_x, plane)
    flat_pot = local_potential.reshape(count_x, plane)
    shift_col = shifts[:, None, None, None]
    potential_plus = flat_pot[None, None] + shift_col
    centre = shift_col + 5.5
    ratio_c = centre / 5.5
    source = -(flat_pert[None] * wave)
    iterate = jnp.zeros_like(source)
    residual = source
    direction = source / centre
    weight = 1.0 / ratio_c
    for repeat in range(APPLY):
        iterate = iterate + direction
        residual = residual - apply_operator(direction, potential_plus, count_x, grid)
        weight_new = 1.0 / (2.0 * ratio_c - weight)
        direction = weight_new * weight * direction + 2.0 * weight_new / 5.5 * residual
        weight = weight_new
    solved = iterate + direction
    scaled_occ = occupations[:, None, None, None] * (4.0 / total_orbitals)
    partial_density = jnp.sum(scaled_occ * wave * solved, axis=0).reshape(
        pert_count, count_x, grid, grid
    )
    band_rows = grid // n_band
    summed = lax.psum(partial_density, "band")
    density = lax.dynamic_slice_in_dim(summed, lax.axis_index("band") * band_rows, band_rows, 2)
    table = cas_table(grid)
    along_z = jnp.einsum("pxyz,zk->pxyk", density, table, precision=highest)
    columns = lax.all_to_all(along_z, "band", split_axis=3, concat_axis=2, tiled=True)
    along_y = jnp.einsum("pxyz,yk->pxzk", columns, table, precision=highest)
    space_cols = grid // n_space
    freq_z = folded(
        lax.axis_index("band") * band_rows + jnp.arange(band_rows, dtype=jnp.int32), grid
    )
    freq_y = folded(
        lax.axis_index("space") * space_cols + jnp.arange(space_cols, dtype=jnp.int32), grid
    )
    freq_x = folded(jnp.arange(grid, dtype=jnp.int32), grid)
    kernel = 256.0 / jnp.sqrt(
        freq_z[:, None, None] ** 2 + freq_y[None, :, None] ** 2 + freq_x[None, None, :] ** 2 + 1.0
    )
    pencil = lax.all_to_all(along_y, "space", split_axis=3, concat_axis=1, tiled=True)
    items = pencil.shape[0]
    flat = pencil.reshape(items, grid, band_rows * space_cols)
    spectral = jnp.einsum("pxm,xj->pmj", flat, table, precision=highest)
    weighted = spectral.reshape(items, band_rows, space_cols, grid) * kernel
    weighted = weighted.reshape(items, band_rows * space_cols, grid)
    restored = jnp.einsum("pmj,jx->pxm", weighted, table, precision=highest)
    restored = restored.reshape(items, grid, band_rows, space_cols)
    returned = lax.all_to_all(restored, "space", split_axis=1, concat_axis=3, tiled=True)
    back_y = jnp.einsum("pxzk,ky->pxzy", returned, table, precision=highest)
    rows_back = lax.all_to_all(back_y, "band", split_axis=3, concat_axis=2, tiled=True)
    back_z = jnp.einsum("pxzy,zk->pxyk", rows_back, table, precision=highest)
    return back_z * (1.0 / float(grid) ** 3)


def solution(mesh):
    in_specs = (
        P("band", "space", None, None),
        P("band"),
        P("band"),
        P(None, "space", None, None),
        P("space", None, None),
    )
    out_specs = P(None, "space", "band", None)
    return jax.shard_map(
        on_device, mesh=mesh, in_specs=in_specs, out_specs=out_specs, check_vma=False
    )
```

profile of v0, /device:TPU:1, one launch (start us, length us, event | category | flops | bytes accessed | tf_op | source)
XLA Modules:
  0.0 541.9 jit_solution(13996261130855419397)
XLA Ops:
  7.2 8.1 %fusion = (f32[1,24,192,192]{3,2,1,0:T(8,128)}, f32[1,24,192,192]{3,2,1,0:T(8,128)}) fusion(f32[1,24,192,192]{3,2,1,0:T(8,128)} %param.8, bf16[1,24,192,192]{3,2,1,0:T(8,128)(2,1)} %param.5, f32[]{:T(128)} %bitcast.1), kind=kLoop, calls=%fused_computation.26 | loop fusion | flops 3538944 | bytes 12386308 | tf_op jit(solution)/shard_map/neg | solution.py:81
  15.2 6.0 %neg.31 = f32[1,1,24,36864]{3,2,1,0:T(8,128)} reshape(f32[1,24,192,192]{3,2,1,0:T(8,128)} %get-tuple-element.107) | data formatting | bytes 7077888 | tf_op jit(solution)/shard_map/neg | solution.py:81
  25.4 3.6 collective-permute-start.1
  28.9 3.9 collective-permute-start
  32.8 4.0 fusion.181
  38.1 4.0 fusion.180
  44.2 3.3 fusion.178
  47.5 4.0 fusion.174
  52.8 4.1 fusion.173
  57.6 3.9 fusion.171
  61.5 4.0 fusion.168
  66.8 4.0 fusion.167
  72.2 3.4 fusion.165
  75.6 3.9 fusion.162
  80.2 4.0 fusion.161
  84.9 4.1 fusion.159
  89.0 15.7 %broadcast_add_fusion = f32[24,192,192]{2,1,0:T(8,128)} fusion(f32[24,192,192]{2,1,0:T(8,128)S(1)} %bitcast.92, f32[]{:T(128)} %bitcast.88), kind=kLoop, calls=%fused_computation.142 | loop fusion | flops 884736 | bytes 7077892 | tf_op jit(solution)/shard_map/add | solution.py:78
  105.5 5.9 %mul.441 = f32[1,1,24,36864]{3,2,1,0:T(8,128)} reshape(f32[1,24,192,192]{3,2,1,0:T(8,128)} %get-tuple-element.108) | data formatting | bytes 7077888 | tf_op jit(solution)/shard_map/mul | solution.py:94
  111.4 6.0 %add.507 = f32[1,1,24,36864]{3,2,1,0:T(8,128)} reshape(f32[24,192,192]{2,1,0:T(8,128)} %broadcast_add_fusion) | data formatting | bytes 7077888 | tf_op jit(solution)/shard_map/add | solution.py:78
  117.5 42.8 %multiply_add_fusion = (f32[1,1,24,36864]{3,2,1,0:T(8,128)}, f32[1,1,24,36864]{3,2,1,0:T(8,128)}) fusion(f32[1,1,24,36864]{3,2,1,0:T(8,128)S(1)} %broadcast_divide_fusion, f32[]{:T(128)} %bitcast.6, f32[]{:T(128)} %bitcast.5, f32[1,1,24,36864]{3,2,1,0:T(8,128)} %neg.31, f32[1,1,24,36864]{3,2,1,0:T(8,128)} %add.507, ...), kind=kLoop, calls=%fused_computation.141 | loop fusion | flops 74317824 | bytes 104103944 | tf_op jit(solution)/shard_map/add | solution.py:90
  162.2 7.1 %fusion.155 = (f32[1,1,24,36672]{3,2,1,0:T(8,128)}, f32[1,1,24,36672]{3,2,1,0:T(8,128)}) fusion(f32[1,1,24,36864]{3,2,1,0:T(8,128)} %get-tuple-element.5), kind=kLoop, calls=%fused_computation.232 | loop fusion | bytes 14082048 | tf_op jit(solution)/shard_map/jit(_roll_static)/slice | solution.py:50
  170.0 4.0 fusion.153
  175.3 4.0 fusion.152
  179.3 3.5 fusion.149
  183.4 4.0 fusion.147
  188.8 3.9 fusion.146
  192.8 4.0 fusion.143
  196.8 4.0 fusion.141
  202.1 3.9 fusion.140
  206.1 3.2 fusion.137
  209.3 3.9 fusion.135
  213.9 3.9 fusion.134
  217.8 5.5 %collective-permute-start.2 = (f32[1,1,4,36864]{3,2,1,0:T(4,128)S(1)}, f32[1,1,4,36864]{3,2,1,0:T(4,128)S(1)}, u32[]{:S(2)}, u32[]{:S(2)}) collective-permute-start(f32[1,1,4,36864]{3,2,1,0:T(4,128)S(1)} %get-tuple-element.55), channel_id=1, source_target_pairs={{1,0},{2,1},{3,2},{4,3},{5,4},{6,5},{7,6},{0,7},{9,8},{10,9},{11,1... | collective-permute-start | bytes 1769480 | tf_op jit(solution)/shard_map/ppermute | solution.py:23
  225.3 10.0 %collective-permute-done.3 = f32[1,1,4,36864]{3,2,1,0:T(4,128)S(1)} collective-permute-done((f32[1,1,4,36864]{3,2,1,0:T(4,128)S(1)}, f32[1,1,4,36864]{3,2,1,0:T(4,128)S(1)}, u32[]{:S(2)}, u32[]{:S(2)}) %collective-permute-start.3) | collective-permute-done | bytes 589856 | tf_op jit(solution)/shard_map/ppermute | solution.py:21
  235.3 9.2 %collective-permute-done.2 = f32[1,1,4,36864]{3,2,1,0:T(4,128)S(1)} collective-permute-done((f32[1,1,4,36864]{3,2,1,0:T(4,128)S(1)}, f32[1,1,4,36864]{3,2,1,0:T(4,128)S(1)}, u32[]{:S(2)}, u32[]{:S(2)}) %collective-permute-start.2) | collective-permute-done | bytes 589856 | tf_op jit(solution)/shard_map/ppermute | solution.py:23
  245.4 42.7 %fusion.16 = f32[1,1,24,36864]{3,2,1,0:T(8,128)} fusion(f32[1,1,24,36864]{3,2,1,0:T(8,128)} %mul.441, f32[1,1,24,36864]{3,2,1,0:T(8,128)} %get-tuple-element.6, f32[1,1,24,36864]{3,2,1,0:T(8,128)S(1)} %copy-done, f32[1,1,4,36864]{3,2,1,0:T(4,128)} %copy-done.1, f32[1,1,4,36864]{3,2,1,0:T(4,128)} %copy-done.2, f32[1,1,24,36672]{3,2,1,0:T(8,128)} %get-tuple-element.52, ...), kind=kLoop, calls=%fused_computation.42 | loop fusion | flops 77856768 | bytes 107642896 | tf_op jit(solution)/shard_map/mul | solution.py:94
  288.1 6.0 %reshape.1912 = f32[1,24,192,192]{3,2,1,0:T(8,128)} reshape(f32[1,1,24,36864]{3,2,1,0:T(8,128)} %fusion.16) | data formatting | bytes 7077888 | tf_op jit(solution)/shard_map/reshape | solution.py:94
  294.1 133.0 %all-reduce.2.cloned.1.call-done = f32[1,24,192,192]{3,2,1,0:T(8,128)} async-done(((f32[1,24,192,192]{3,2,1,0:T(8,128)}), f32[1,24,192,192]{3,2,1,0:T(8,128)}) %all-reduce.2.cloned.1.call-update) | async-done | bytes 3538960 | tf_op jit(solution)/shard_map/psum | solution.py:98
  431.0 3.6 reduce
  436.2 6.2 %all-to-all-start = ((f32[16,1,3456]{2,1,0:T(1,128)}), f32[16,1,3456]{2,1,0:T(1,128)S(1)}, u32[]{:S(2)}, u32[]{:S(2)}) async-start(f32[16,1,3456]{2,1,0:T(1,128)} %reshape.1919), calls=%async_computation | async-start | bytes 442368 | tf_op jit(solution)/shard_map/all_to_all | solution.py:102
  442.5 6.8 %all-to-all-done = f32[16,1,3456]{2,1,0:T(1,128)S(1)} async-done(((f32[16,1,3456]{2,1,0:T(1,128)}), f32[16,1,3456]{2,1,0:T(1,128)S(1)}, u32[]{:S(2)}, u32[]{:S(2)}) %all-to-all-start) | async-done | bytes 221216 | tf_op jit(solution)/shard_map/all_to_all | solution.py:102
  458.8 3.6 reduce.2
  464.0 6.5 %all-to-all-start.1 = ((f32[8,1,6912]{2,1,0:T(1,128)}), f32[8,1,6912]{2,1,0:T(1,128)S(1)}, u32[]{:S(2)}, u32[]{:S(2)}) async-start(f32[8,1,6912]{2,1,0:T(1,128)} %reshape.1921), calls=%async_computation.1 | async-start | bytes 442368 | tf_op jit(solution)/shard_map/all_to_all | solution.py:115
  470.6 7.3 %all-to-all-done.1 = f32[8,1,6912]{2,1,0:T(1,128)S(1)} async-done(((f32[8,1,6912]{2,1,0:T(1,128)}), f32[8,1,6912]{2,1,0:T(1,128)S(1)}, u32[]{:S(2)}, u32[]{:S(2)}) %all-to-all-start.1) | async-done | bytes 221216 | tf_op jit(solution)/shard_map/all_to_all | solution.py:115
  486.6 3.6 reduce.4
  491.1 10.2 %all_to_all.60 = f32[8,1,6912]{2,1,0:T(1,128)S(1)} all-to-all(f32[8,1,6912]{2,1,0:T(1,128)S(1)} %reshape.1923), channel_id=1, replica_groups=mesh['band'=16,'space'=8] {'space'}, dimensions={0} | all-to-all | bytes 442368 | tf_op jit(solution)/shard_map/all_to_all | solution.py:123
  507.6 3.6 reduce.6
  512.1 13.1 %all_to_all.61 = f32[16,1,3456]{2,1,0:T(1,128)S(1)} all-to-all(f32[16,1,3456]{2,1,0:T(1,128)S(1)} %reshape.1925), channel_id=1, replica_groups=mesh['band'=16,'space'=8] {'band'}, dimensions={0} | all-to-all | bytes 442368 | tf_op jit(solution)/shard_map/all_to_all | solution.py:125
  (91 shorter events, 67.2 us)
Async XLA Ops:
  6.5 420.6 %all-reduce.2.cloned.1.call-start = ((), (), s32[]{:S(2)}) async-start(), calls=%async_computation.4 | async-start | bytes 9437184 | tf_op jit(solution)/shard_map/psum | solution.py:98
  25.4 92.2 %collective-permute-start.1 = (f32[1,1,4,36864]{3,2,1,0:T(4,128)}, f32[1,1,4,36864]{3,2,1,0:T(4,128)}, u32[]{:S(2)}, u32[]{:S(2)}) collective-permute-start(f32[1,1,4,36864]{3,2,1,0:T(4,128)} %get-tuple-element.94), channel_id=1, source_target_pairs={{0,1},{1,2},{2,3},{3,4},{4,5},{5,6},{6,7},{7,0},{8,9},{9,10},{10,1... | collective-permute-start | bytes 1769480 | tf_op jit(solution)/shard_map/ppermute | solution.py:21
  28.9 88.6 %collective-permute-start = (f32[1,1,4,36864]{3,2,1,0:T(4,128)}, f32[1,1,4,36864]{3,2,1,0:T(4,128)}, u32[]{:S(2)}, u32[]{:S(2)}) collective-permute-start(f32[1,1,4,36864]{3,2,1,0:T(4,128)} %get-tuple-element.93), channel_id=1, source_target_pairs={{1,0},{2,1},{3,2},{4,3},{5,4},{6,5},{7,6},{0,7},{9,8},{10,9},{11,1... | collective-permute-start | bytes 1769480 | tf_op jit(solution)/shard_map/ppermute | solution.py:23
  80.2 8.8 %slice-start = ((s8[4718592]{0:T(1024)(128)(4,1)}), s8[4194304]{0:T(1024)(128)(4,1)S(1)}, s32[]{:S(2)}) async-start(s8[4718592]{0:T(1024)(128)(4,1)} %bitcast.91), calls=%async_computation.5 | async-start | bytes 8388608
  84.2 4.8 slice-start.1
  117.5 42.9 %copy-start.3 = (pred[36864]{0:T(1024)(128)(4,1)}, pred[36864]{0:T(1024)(128)(4,1)S(1)}, u32[]{:S(2)}) copy-start(pred[36864]{0:T(1024)(128)(4,1)S(1)} %get-tuple-element.115) | copy-start | bytes 110596
  117.5 42.9 %copy-start.4 = (pred[36864]{0:T(1024)(128)(4,1)}, pred[36864]{0:T(1024)(128)(4,1)S(1)}, u32[]{:S(2)}) copy-start(pred[36864]{0:T(1024)(128)(4,1)S(1)} %get-tuple-element.116) | copy-start | bytes 110596
  162.2 7.1 %copy-start = (f32[1,1,24,36864]{3,2,1,0:T(8,128)S(1)}, f32[1,1,24,36864]{3,2,1,0:T(8,128)}, u32[]{:S(2)}) copy-start(f32[1,1,24,36864]{3,2,1,0:T(8,128)} %get-tuple-element.5) | copy-start | bytes 10616836
  217.8 17.5 %collective-permute-start.3 = (f32[1,1,4,36864]{3,2,1,0:T(4,128)S(1)}, f32[1,1,4,36864]{3,2,1,0:T(4,128)S(1)}, u32[]{:S(2)}, u32[]{:S(2)}) collective-permute-start(f32[1,1,4,36864]{3,2,1,0:T(4,128)S(1)} %get-tuple-element.56), channel_id=1, source_target_pairs={{0,1},{1,2},{2,3},{3,4},{4,5},{5,6},{6,7},{7,0},{8,9},{9,10},{10,1... | collective-permute-start | bytes 1769480 | tf_op jit(solution)/shard_map/ppermute | solution.py:21
  217.8 26.7 %collective-permute-start.2 = (f32[1,1,4,36864]{3,2,1,0:T(4,128)S(1)}, f32[1,1,4,36864]{3,2,1,0:T(4,128)S(1)}, u32[]{:S(2)}, u32[]{:S(2)}) collective-permute-start(f32[1,1,4,36864]{3,2,1,0:T(4,128)S(1)} %get-tuple-element.55), channel_id=1, source_target_pairs={{1,0},{2,1},{3,2},{4,3},{5,4},{6,5},{7,6},{0,7},{9,8},{10,9},{11,1... | collective-permute-start | bytes 1769480 | tf_op jit(solution)/shard_map/ppermute | solution.py:23
  235.3 9.2 %copy-start.1 = (f32[1,1,4,36864]{3,2,1,0:T(4,128)}, f32[1,1,4,36864]{3,2,1,0:T(4,128)S(1)}, u32[]{:S(2)}) copy-start(f32[1,1,4,36864]{3,2,1,0:T(4,128)S(1)} %collective-permute-done.3) | copy-start | bytes 1769476
  244.6 0.8 copy-start.2
  436.2 13.1 %all-to-all-start = ((f32[16,1,3456]{2,1,0:T(1,128)}), f32[16,1,3456]{2,1,0:T(1,128)S(1)}, u32[]{:S(2)}, u32[]{:S(2)}) async-start(f32[16,1,3456]{2,1,0:T(1,128)} %reshape.1919), calls=%async_computation | async-start | bytes 442368 | tf_op jit(solution)/shard_map/all_to_all | solution.py:102
  464.0 13.9 %all-to-all-start.1 = ((f32[8,1,6912]{2,1,0:T(1,128)}), f32[8,1,6912]{2,1,0:T(1,128)S(1)}, u32[]{:S(2)}, u32[]{:S(2)}) async-start(f32[8,1,6912]{2,1,0:T(1,128)} %reshape.1921), calls=%async_computation.1 | async-start | bytes 442368 | tf_op jit(solution)/shard_map/all_to_all | solution.py:115
Sparse Core Ops, SparseCore 0:
  294.2 132.8 all-reduce.1
where the time goes:
time: 545 us; the launch traced here: 542 us
  local copies, waits for them, and re-layouts  170 us (31%)
  waiting for transfers between devices  166 us (30%)
  other arithmetic  133 us (24%)
  starting transfers between devices  25.6 us (5%)
  blocking collectives  23.2 us (4%)
  between operations  15.7 us (3%)
  matrix products  8.14 us (1%)
    psum x1, waiting for transfers between devices, on_device(): summed = lax.psum(partial_density, 'band')  133 us
    add x1, other arithmetic, on_device(): weight_new * weight * direction + 2.0 * weight_new / 5.5 * residual  42.8 us
    mul x1, other arithmetic, on_device(): scaled_occ * wave * solved  42.7 us
    slice x8, local copies, waits for them, and re-layouts, apply_operator(): jnp.roll(direction, -offset * grid, 3)  20.5 us
    slice x8, local copies, waits for them, and re-layouts, apply_operator(): jnp.roll(direction, offset, 3)  18.7 us
    slice x8, local copies, waits for them, and re-layouts, apply_operator(): jnp.roll(direction, -offset, 3)  18.6 us
    slice x8, local copies, waits for them, and re-layouts, apply_operator(): jnp.roll(direction, offset - grid, 3)  18.6 us
    slice x8, local copies, waits for them, and re-layouts, apply_operator(): jnp.roll(direction, grid - offset, 3)  18.5 us
  transfers between devices with their start and end apart: 7, of which 5 were waited for; matrix products, arithmetic and copies ran while one was open for 16% of the time, Pallas kernels for 0%

commit v1 on v0

v1 whole, which is shorter than its diff:
```python
import functools
import math

import jax
import jax.numpy as jnp
import numpy as np
from jax import lax
from jax.experimental import pallas as pl
from jax.experimental.pallas import tpu as pltpu
from jax.sharding import PartitionSpec as P

MESH = pl.DeviceIdType.MESH
BF16 = jnp.bfloat16
F32 = jnp.float32
NG = 192
SLAB = 24
EXT = 32
COEFFS = (-205.0 / 72.0, 8.0 / 5.0, -1.0 / 5.0, 8.0 / 315.0, -1.0 / 560.0)
WEIGHTS = (8064.0, -1008.0, 128.0, -9.0)
ROWS = 288
PIECE = 4 * ROWS // 8


def cas(product):
    angles = (np.asarray(product, np.int64) % NG).astype(np.float64) * (2.0 * math.pi / NG)
    return np.cos(angles) + np.sin(angles)


def halves(table):
    table = np.asarray(table, np.float32)
    high = table.astype(jnp.bfloat16)
    low = (table - high.astype(np.float32)).astype(jnp.bfloat16)
    return np.stack([high, low])


def tables():
    index = np.arange(NG)
    plain = cas(index[:, None] * index[None, :])
    stencil = np.zeros((NG, NG), np.float32)
    for offset, weight in enumerate(WEIGHTS, 1):
        for sign in (1, -1):
            stencil[index, (index + sign * offset) % NG] += weight
    forward_z = halves(plain).reshape(2 * NG, NG)
    forward_y = np.zeros((2, 256, 256))
    for layer in range(2):
        forward_y[layer, :128, :NG] = plain[:128]
        forward_y[layer, 128 + 64 * layer : 192 + 64 * layer, :NG] = plain[128:]
    forward_x = np.zeros((NG, 256))
    for core in range(2):
        for space in range(8):
            for slot in range(16):
                step, layer = divmod(slot, 2)
                ext = (14 - 2 * step if core == 0 else 16 + 2 * step) + layer
                x = (SLAB * space + ext - 4) % NG
                forward_x[:, (core * 8 + space) * 16 + slot] = plain[:, x]
    inverse_y = np.zeros((256, 256))
    inverse_z = np.zeros((256, NG))
    for band in range(16):
        inverse_y[band * 16 : band * 16 + 12, :NG] = plain[band * 12 : band * 12 + 12]
        x_lo, y, core = band // 8, (band // 2) % 4, band % 2
        first = 24 * (2 * y + x_lo) + 12 * core
        inverse_z[band * 16 : band * 16 + 12] = plain[first : first + 12]
    return (
        stencil.astype(jnp.bfloat16),
        forward_z,
        halves(forward_y),
        halves(forward_x),
        halves(plain),
        halves(inverse_y),
        halves(inverse_z),
    )


def split(value):
    high = value.astype(BF16)
    low = (value - high.astype(F32)).astype(BF16)
    return high, low


def dot(a, b, dims=((1,), (0,))):
    return lax.dot_general(a, b, (dims, ((), ())), preferred_element_type=F32)


def dot3_table_left(table, value, dims=((1,), (0,))):
    high, low = split(value)
    return dot(table[0], high, dims) + (dot(table[1], high, dims) + dot(table[0], low, dims))


def dot3_table_right(value, table):
    high, low = split(value)
    return dot(high, table[0]) + (dot(low, table[0]) + dot(high, table[1]))


def pack_into(ref, index, layer):
    ref[index, :NG, :] = layer[:, :128]
    ref[index, NG:, :64] = layer[:96, 128:]
    ref[index, NG:, 64:] = layer[96:, 128:]


def unpacked(ref, row):
    main = ref[pl.ds(row, NG), :]
    tail = ref[pl.ds(row + NG, 96), :]
    return main, tail


def kernel(
    coef, orb_hbm, pert_hbm, pot_hbm, stencil, tab_z, tab_fy, tab_fx, tab_p, tab_iy, tab_iz, out,
    orb, pert, pot, v, e,
    osend, orecv, psend, precv, pout,
    mine, other, crecv, yrecv, xsum, xrecv, red,
    gsend, grecv, wsend, wrecv, brow, zsend, zrecv, mat,
    load_sem, osem, psem, fsem, csem, ysem, xsem, gsem, wsem, zsem,
):
    band = lax.axis_index("band")
    space = lax.axis_index("space")
    core = lax.rem(band, 2)
    y = lax.rem(band // 2, 4)
    x_lo = band // 8
    group = 2 * y + x_lo
    up = lax.rem(space + 1, 8)
    down = lax.rem(space + 7, 8)

    def band_of(x, yy, c):
        return x * 8 + yy * 2 + c

    def y_at(k):
        return lax.rem(y + k, 4)

    loads = []
    for number, (src, dst, lead, lo, hi) in enumerate(
        (
            (pert_hbm, pert, True, 0, 4),
            (pert_hbm, pert, True, 20, 24),
            (orb_hbm, orb, True, 0, 4),
            (orb_hbm, orb, True, 20, 24),
            (orb_hbm, orb, True, 4, 20),
            (pert_hbm, pert, True, 4, 20),
            (pot_hbm, pot, False, 0, 24),
        )
    ):
        source = src.at[0, lo:hi] if lead else src.at[lo:hi]
        target = dst.at[4 + lo : 4 + hi] if dst is not pot else dst.at[lo:hi]
        copy = pltpu.make_async_copy(source, target, load_sem.at[number])
        copy.start()
        loads.append(copy)

    barrier = pltpu.get_barrier_semaphore()
    for k in range(1, 16):
        pl.semaphore_signal(
            barrier, inc=1, device_id=(lax.rem(band + k, 16), space), device_id_type=MESH
        )
    for k in range(1, 8):
        for c in range(2):
            pl.semaphore_signal(
                barrier,
                inc=1,
                device_id=(band_of(x_lo, y, c), lax.rem(space + k, 8)),
                device_id_type=MESH,
            )

    for layer in list(range(0, 8)) + list(range(32, 40)):
        e[layer] = jnp.zeros((NG, NG), F32)

    piece = 2 * y + core
    piece_row = pl.multiple_of(piece * PIECE, 8)
    half_row = pl.multiple_of(lax.rem(piece, 2) * PIECE, 8)
    loads[0].wait()
    loads[1].wait()
    pack_into(psend, 0, pert[24 + piece // 2])
    pack_into(psend, 1, pert[4 + piece // 2])
    loads[2].wait()
    loads[3].wait()

    pl.semaphore_wait(barrier, 29)

    pcopies, ocopies = [], {}
    for way, target in ((0, up), (1, down)):
        copy = pltpu.make_async_remote_copy(
            src_ref=psend.at[way, pl.ds(half_row, PIECE)],
            dst_ref=precv.at[way, pl.ds(piece_row, PIECE)],
            send_sem=psem.at[0, way],
            recv_sem=psem.at[1, way],
            device_id=(band, target),
            device_id_type=MESH,
        )
        copy.start()
        pcopies.append(copy)
    for near in range(4):
        for way, target in ((0, up), (1, down)):
            layer = 3 - near if way == 0 else near
            pack_into(
                osend.at[way], layer, orb[(24 if way == 0 else 4) + layer].astype(F32)
            )
            copy = pltpu.make_async_remote_copy(
                src_ref=osend.at[way, layer],
                dst_ref=orecv.at[way, layer],
                send_sem=osem.at[0, way, layer],
                recv_sem=osem.at[1, way, layer],
                device_id=(band, target),
                device_id_type=MESH,
            )
            copy.start()
            ocopies[way, layer] = copy

    def forwards(way):
        copies = []
        for other_piece in range(1, 8):
            to = lax.rem(piece + other_piece, 8)
            copies.append(
                pltpu.make_async_remote_copy(
                    src_ref=precv.at[way, pl.ds(piece_row, PIECE)],
                    dst_ref=precv.at[way, pl.ds(piece_row, PIECE)],
                    send_sem=fsem.at[0, way, other_piece],
                    recv_sem=fsem.at[1, way, other_piece],
                    device_id=(band_of(x_lo, to // 2, lax.rem(to, 2)), space),
                    device_id_type=MESH,
                )
            )
        return copies

    a_own, b_own, b_sten, q_shift = coef[0], coef[1], coef[2], coef[3]
    g0, g1, beta, beta_sten, factor = coef[4], coef[5], coef[6], coef[7], coef[8]

    loads[4].wait()
    loads[5].wait()
    loads[6].wait()

    def make_v(layer, carry):
        v[layer] = orb[layer].astype(F32) * pert[layer]
        return carry

    lax.fori_loop(4, 28, make_v, 0)

    def shifted(ref, layer):
        value = ref[layer]
        high, low = split(value)
        total = WEIGHTS[0] * (ref[layer - 1] + ref[layer + 1])
        for offset in range(2, 5):
            total += WEIGHTS[offset - 1] * (ref[layer - offset] + ref[layer + offset])
        total += dot(high, stencil[...]) + dot(low, stencil[...])
        total += dot(stencil[...], high) + dot(stencil[...], low)
        return value, total

    def make_e(layer, carry):
        value, total = shifted(v, layer + 4)
        diagonal = pot[layer] + q_shift
        e[layer + 8] = (a_own - b_own * diagonal) * value + b_sten * total
        return carry

    def transformed(layer):
        value, total = shifted(e, layer + 4)
        own = jnp.logical_and(layer >= 4, layer < 28)
        diagonal = pot[jnp.clip(layer - 4, 0, SLAB - 1)] + q_shift
        base = jnp.where(own, g0, 0.0)
        solved = base * v[layer] + (g1 - beta * diagonal) * value + beta_sten * total
        density = factor * orb[layer].astype(F32) * solved
        high, low = split(density)
        last = ((1,), (1,))
        both = dot(tab_z[...], high, last)
        return both[:NG] + (both[NG:] + dot(tab_z[:NG], low, last))

    def make_pair(ref, index, base):
        first = transformed(base)
        ref[index, 0] = first[:, :128]
        ref[index, 2, :, :64] = first[:, 128:]
        second = transformed(base + 1)
        ref[index, 1] = second[:, :128]
        ref[index, 2, :, 64:] = second[:, 128:]

    def base_of(c, j):
        return jnp.where(c == 0, 14 - 2 * j, 16 + 2 * j)

    def core_copy(j):
        return pltpu.make_async_remote_copy(
            src_ref=other.at[j],
            dst_ref=crecv.at[j],
            send_sem=csem.at[0, j],
            recv_sem=csem.at[1, j],
            device_id=(band_of(x_lo, y, 1 - core), space),
            device_id_type=MESH,
        )

    def y_copy(j, k):
        row = pl.multiple_of(48 * y_at(k), 8)
        return pltpu.make_async_remote_copy(
            src_ref=mine.at[j, :, pl.ds(row, 48)],
            dst_ref=yrecv.at[k - 1, j],
            send_sem=ysem.at[0, k - 1, j],
            recv_sem=ysem.at[1, k - 1, j],
            device_id=(band_of(x_lo, y_at(k), core), space),
            device_id_type=MESH,
        )

    def x_copy(j):
        row = pl.multiple_of(24 * (1 - x_lo), 8)
        return pltpu.make_async_remote_copy(
            src_ref=xsum.at[j, :, pl.ds(row, 24)],
            dst_ref=xrecv.at[j],
            send_sem=xsem.at[0, j],
            recv_sem=xsem.at[1, j],
            device_id=(band_of(1 - x_lo, y, core), space),
            device_id_type=MESH,
        )

    def compute_step(j):
        make_pair(other, j, base_of(1 - core, j))
        core_copy(j).start()
        make_pair(mine, j, base_of(core, j))

    def reduce_core(j):
        core_copy(j).wait_recv()
        mine[j] += crecv[j]
        for k in (2, 1, 3):
            y_copy(j, k).start()

    def reduce_y(j):
        for k in (1, 2, 3):
            y_copy(j, k).wait_recv()
        row = pl.multiple_of(48 * y, 8)
        xsum[j] = (mine[j, :, pl.ds(row, 48)] + yrecv[0, j]) + (yrecv[1, j] + yrecv[2, j])
        x_copy(j).start()

    def reduce_x(j):
        x_copy(j).wait_recv()
        row = pl.multiple_of(24 * x_lo, 8)
        red[j] = xsum[j, :, pl.ds(row, 24)] + xrecv[j]

    def step(j, carry):
        @pl.when(j < 8)
        def _():
            compute_step(j)

        @pl.when(jnp.logical_and(j >= 1, j < 9))
        def _():
            reduce_core(j - 1)

        @pl.when(jnp.logical_and(j >= 3, j < 11))
        def _():
            reduce_y(j - 3)

        @pl.when(j >= 4)
        def _():
            reduce_x(j - 4)

        return carry

    forward = {}
    for way in range(2):
        pcopies[way].wait_recv()
        forward[way] = forwards(way)
        for copy in forward[way]:
            copy.start()

    lax.fori_loop(4, 20, make_e, 0)
    lax.fori_loop(0, 2, step, 0)

    for way in range(2):
        for copy in forward[way]:
            copy.wait_recv()
        for layer in range(4):
            ocopies[way, layer].wait_recv()
            at = layer + (0 if way == 0 else 28)
            main, tail = unpacked(orecv.at[way, layer], 0)
            pmain, ptail = unpacked(precv.at[way], layer * ROWS)
            orb[at, :, :128] = main.astype(BF16)
            orb[at, :96, 128:] = tail[:, :64].astype(BF16)
            orb[at, 96:, 128:] = tail[:, 64:].astype(BF16)
            main = main * pmain
            tail = tail * ptail
            v[at, :, :128] = main
            v[at, :96, 128:] = tail[:, :64]
            v[at, 96:, 128:] = tail[:, 64:]

    lax.fori_loop(0, 4, make_e, 0)
    lax.fori_loop(20, 24, make_e, 0)
    lax.fori_loop(2, 12, step, 0)

    red0 = jnp.concatenate([red[:, 0].reshape(NG, 128), red[:, 2].reshape(NG, 128)], axis=1)
    red1 = jnp.concatenate([red[:, 1].reshape(NG, 128), red[:, 2].reshape(NG, 128)], axis=1)
    for layer, value in enumerate((red0, red1)):
        high, low = split(value)
        table_high, table_low = tab_fy[0, layer], tab_fy[1, layer]
        columns = dot(high, table_high) + (dot(low, table_high) + dot(high, table_low))
        for j in range(8):
            for half in range(2):
                gsend[pl.ds(half * 16 + 2 * j + layer, 24, stride=32), :] = columns[
                    24 * j : 24 * j + 24, 128 * half : 128 * half + 128
                ]

    mine_at = core * 8 + space

    def g_copy(k, c):
        to_space = lax.rem(space + k, 8)
        to_core = lax.rem(core + c, 2)
        row = pl.multiple_of(48 * (to_core * 8 + to_space), 8)
        return pltpu.make_async_remote_copy(
            src_ref=gsend.at[pl.ds(row, 48)],
            dst_ref=grecv.at[mine_at],
            send_sem=gsem.at[0, k, c],
            recv_sem=gsem.at[1, k, c],
            device_id=(band_of(x_lo, y, to_core), to_space),
            device_id_type=MESH,
        )

    partners = [(k, c) for k in (4, 3, 5, 2, 6, 1, 7, 0) for c in range(2) if (k, c) != (0, 0)]
    for k, c in partners:
        g_copy(k, c).start()
    grecv[mine_at] = gsend[pl.ds(pl.multiple_of(48 * mine_at, 8), 48), :]

    kx = lax.broadcasted_iota(jnp.int32, (NG, 128), 0)
    lane = lax.broadcasted_iota(jnp.int32, (NG, 128), 1)
    gx = jnp.minimum(kx, NG - kx)
    factors = []
    for unit in range(3):
        number = 3 * mine_at + unit
        kz = 24 * group + number // 2
        gz = jnp.minimum(kz, NG - kz)
        ky = lane + 128 * lax.rem(number, 2)
        gy = jnp.minimum(ky, NG - ky)
        square = (gx * gx + gy * gy + (gz * gz + 1)).astype(F32)
        factors.append((256.0 / float(NG) ** 3) / jnp.sqrt(square))
    coulomb = jnp.concatenate(factors, axis=1)

    for k, c in partners:
        g_copy(k, c).wait_recv()
    pencil = jnp.concatenate(
        [grecv[:, 16 * unit : 16 * unit + 16, :].reshape(256, 128) for unit in range(3)], axis=1
    )
    spectral = dot3_table_left(tab_fx, pencil) * coulomb
    restored = dot3_table_left(tab_p, spectral)
    for unit in range(3):
        wsend[unit] = restored[:, 128 * unit : 128 * unit + 128]

    def w_copy(k):
        to_space = lax.rem(space + k, 8)
        row = pl.multiple_of(24 * to_space, 8)
        return pltpu.make_async_remote_copy(
            src_ref=wsend.at[:, pl.ds(row, 24)],
            dst_ref=wrecv.at[pl.ds(3 * space, 3)],
            send_sem=wsem.at[0, k],
            recv_sem=wsem.at[1, k],
            device_id=(band, to_space),
            device_id_type=MESH,
        )

    for k in (4, 3, 5, 2, 6, 1, 7):
        w_copy(k).start()
    wrecv[pl.ds(3 * space, 3)] = wsend[:, pl.ds(pl.multiple_of(24 * space, 8), 24), :]
    brow[...] = jnp.zeros(brow.shape, F32)
    for k in (4, 3, 5, 2, 6, 1, 7):
        w_copy(k).wait_recv()

    for unit in range(24):
        brow[unit % 2, pl.ds(unit // 2, 24, stride=16), :] = wrecv[unit]
    rows = jnp.concatenate([brow[0], brow[1]], axis=1)
    zsend[...] = dot3_table_left(tab_iy, rows, ((1,), (1,)))

    def z_copy(k):
        to = lax.rem(band + k, 16)
        return pltpu.make_async_remote_copy(
            src_ref=zsend.at[pl.ds(pl.multiple_of(16 * to, 8), 16)],
            dst_ref=zrecv.at[band],
            send_sem=zsem.at[0, k],
            recv_sem=zsem.at[1, k],
            device_id=(to, space),
            device_id_type=MESH,
        )

    order = (4, 12, 8, 3, 5, 11, 13, 2, 6, 10, 14, 7, 9, 1, 15)
    for k in order:
        z_copy(k).start()
    zrecv[band] = zsend[pl.ds(pl.multiple_of(16 * band, 8), 16), :]
    for k in order:
        z_copy(k).wait_recv()

    granule = lax.broadcasted_iota(jnp.int32, (16, 128), 1) // 16
    for third in range(3):
        for part in range(2):
            blocks = [zrecv[8 * part + i, :, 128 * third : 128 * third + 128] for i in range(8)]
            for bit in (1, 2, 4):
                upper = lax.rem(granule // bit, 2) == 1
                after = list(blocks)
                for i in range(8):
                    if not i & bit:
                        low, high = blocks[i], blocks[i | bit]
                        after[i] = jnp.where(upper, pltpu.roll(high, 16 * bit, 1), low)
                        after[i | bit] = jnp.where(upper, high, pltpu.roll(low, 128 - 16 * bit, 1))
                blocks = after
            for i in range(8):
                x = 8 * third + i
                mat[16 * x : 16 * x + 16, 128 * part : 128 * part + 128] = blocks[i]
    result = dot3_table_right(mat[...], tab_iz)
    for x in range(SLAB):
        out[0, x] = result[16 * x : 16 * x + 12]

    for way in range(2):
        pcopies[way].wait_send()
        for copy in forward[way]:
            copy.wait_send()
        for layer in range(4):
            ocopies[way, layer].wait_send()

    def drain(j, carry):
        core_copy(j).wait_send()
        for k in (1, 2, 3):
            y_copy(j, k).wait_send()
        x_copy(j).wait_send()
        return carry

    lax.fori_loop(0, 8, drain, 0)
    for k, c in partners:
        g_copy(k, c).wait_send()
    for k in (4, 3, 5, 2, 6, 1, 7):
        w_copy(k).wait_send()
    for k in order:
        z_copy(k).wait_send()


def scalars(occupations, shifts):
    delta = 5.5
    shift = shifts[0]
    theta = shift + 5.5
    ratio = theta / delta
    w0 = 1.0 / ratio
    w1 = 1.0 / (2.0 * ratio - w0)
    w2 = 1.0 / (2.0 * ratio - w1)
    alpha1, beta1 = w1 * w0, 2.0 * w1 / delta
    alpha2, beta2 = w2 * w1, 2.0 * w2 / delta
    a = alpha1 / theta + beta1
    b = beta1 / theta
    g0 = (1.0 - w2 * w0) / theta
    g1 = 1.0 + alpha2 + beta2 / beta1
    q_shift = shift - 1.5 * COEFFS[0]
    factor = -occupations[0] * (4.0 / 16.0)
    return jnp.stack([a, b, b / 10080.0, q_shift, g0, g1, beta2, beta2 / 10080.0, factor])


def on_device(orbitals, occupations, shifts, perturbations, local_potential):
    consts = tables()
    any_space = pl.BlockSpec(memory_space=pl.ANY)
    vmem = pl.BlockSpec(memory_space=pltpu.VMEM)
    dma = pltpu.SemaphoreType.DMA
    return pl.pallas_call(
        kernel,
        out_shape=jax.ShapeDtypeStruct((1, SLAB, 12, NG), F32),
        in_specs=[pl.BlockSpec(memory_space=pltpu.SMEM)] + [any_space] * 3 + [vmem] * 7,
        out_specs=vmem,
        scratch_shapes=[
            pltpu.VMEM((EXT, NG, NG), BF16),
            pltpu.VMEM((EXT, NG, NG), F32),
            pltpu.VMEM((SLAB, NG, NG), F32),
            pltpu.VMEM((EXT, NG, NG), F32),
            pltpu.VMEM((EXT + 8, NG, NG), F32),
            pltpu.VMEM((2, 4, ROWS, 128), F32),
            pltpu.VMEM((2, 4, ROWS, 128), F32),
            pltpu.VMEM((2, ROWS, 128), F32),
            pltpu.VMEM((2, 4 * ROWS, 128), F32),
            pltpu.VMEM((8, 128), F32),
            pltpu.VMEM((8, 3, NG, 128), F32),
            pltpu.VMEM((8, 3, NG, 128), F32),
            pltpu.VMEM((8, 3, NG, 128), F32),
            pltpu.VMEM((3, 8, 3, 48, 128), F32),
            pltpu.VMEM((8, 3, 48, 128), F32),
            pltpu.VMEM((8, 3, 24, 128), F32),
            pltpu.VMEM((8, 3, 24, 128), F32),
            pltpu.VMEM((768, 128), F32),
            pltpu.VMEM((16, 48, 128), F32),
            pltpu.VMEM((3, NG, 128), F32),
            pltpu.VMEM((24, 24, 128), F32),
            pltpu.VMEM((2, 384, 128), F32),
            pltpu.VMEM((256, 384), F32),
            pltpu.VMEM((16, 16, 384), F32),
            pltpu.VMEM((384, 256), F32),
            dma((7,)),
            dma((2, 2, 4)),
            dma((2, 2)),
            dma((2, 2, 8)),
            dma((2, 8)),
            dma((2, 3, 8)),
            dma((2, 8)),
            dma((2, 8, 2)),
            dma((2, 8)),
            dma((2, 16)),
        ],
        compiler_params=pltpu.CompilerParams(
            collective_id=0, has_side_effects=True, vmem_limit_bytes=60 * 2**20
        ),
        name="response",
    )(scalars(occupations, shifts), orbitals, perturbations, local_potential, *map(jnp.asarray, consts))


def solution(mesh):
    in_specs = (
        P("band", "space", None, None),
        P("band"),
        P("band"),
        P(None, "space", None, None),
        P("space", None, None),
    )
    out_specs = P(None, "space", "band", None)
    return jax.shard_map(
        on_device, mesh=mesh, in_specs=in_specs, out_specs=out_specs, check_vma=False
    )
```

time: 545 us -> 101 us (0.19)
  local copies, waits for them, and re-layouts: 170 us -> 2.55 us
  waiting for transfers between devices: 166 us -> 0 us
  other arithmetic: 133 us -> 0 us
  Pallas kernels: 0 us -> 96.3 us
  starting transfers between devices: 25.6 us -> 0 us
  blocking collectives: 23.2 us -> 0 us
  between operations: 15.7 us -> 1.6 us
  matrix products: 8.14 us -> 0 us
    psum x1 -> x0, waiting for transfers between devices: 133 us -> none  [on_device(): summed = lax.psum(partial_density, 'band')]
    slice x50 -> x0, local copies, waits for them, and re-layouts: 115 us -> none  [the longest x8 20.5 us: apply_operator(): jnp.roll(direction, -offset * grid, 3)]
    pallas_call x0 -> x1, Pallas kernels: none -> 96.3 us  [on_device(): pl.pallas_call(kernel, out_shape=jax.ShapeDtypeStruct((1, SLAB, 12, NG),...]
    add x3 -> x0, other arithmetic: 58.6 us -> none  [the longest x1 42.8 us: on_device(): weight_new * weight * direction + 2.0 * weight_new / 5.5 * residual]
    mul x1 -> x0, other arithmetic: 42.7 us -> none  [on_device(): scaled_occ * wave * solved]
    all_to_all x2 -> x0, blocking collectives: 23.2 us -> none  [the longest x1 13.1 us: on_device(): lax.all_to_all(back_y, 'band', split_axis=3, concat_axis=2, tiled=True)]
    ppermute x4 -> x0, waiting for transfers between devices: 19.2 us -> none  [the longest x2 10 us: padded_2(): lax.ppermute(tail, axis, [(i, (i + 1) % count) for i in range(count)])]
    unnamed x23 -> x0, local copies, waits for them, and re-layouts: 14.5 us -> none
  transfers between devices with their start and end apart: 7 -> 0, of which waited for: 5 -> 0; matrix products, arithmetic and copies ran while one was open for 16% -> 0% of each run, Pallas kernels for 0% -> 0%
where the time goes in v1:
time: 101 us; the launch traced here: 100 us
  Pallas kernels  96.3 us (95%)
  local copies, waits for them, and re-layouts  2.55 us (3%)
  between operations  1.6 us (2%)
    pallas_call x1, Pallas kernels, on_device(): pl.pallas_call(kernel, out_shape=jax.ShapeDtypeStruct((1, SLAB, 12, NG),...  96.3 us

profile of v1, /device:TPU:1, one launch (start us, length us, event | category | flops | bytes accessed | tf_op | source)
XLA Modules:
  0.0 100.4 jit_solution(1634710320697546103)
XLA Ops:
  1.6 0.7 stack.33.coef
  2.3 96.3 %response.1 = f32[1,24,12,192]{3,2,1,0:T(8,128)} custom-call(f32[9]{0:T(128)} %stack.33.coef, bf16[1,24,192,192]{3,2,1,0:T(8,128)(2,1)} %orb_hbm.1, f32[1,24,192,192]{3,2,1,0:T(8,128)} %pert_hbm.1, f32[24,192,192]{2,1,0:T(8,128)} %pot_hbm.1, bf16[192,192]{1,0:T(8,128)(2,1)} %constant.41.clone.stencil, bf16[384,192]{1,0:T(8,128)(2,1)} %constant.42.clone.tab_z, ...), custom_call_target="tpu_custom_call" | custom-call | tf_op jit(solution)/shard_map/response/pallas_call | solution.py:543
  98.5 1.9 %copy.13 = f32[1,24,12,192]{3,1,2,0:T(8,128)} copy(f32[1,24,12,192]{3,2,1,0:T(8,128)} %response.1) | data formatting | bytes 442368 | tf_op jit(solution)/shard_map/response/pallas_call | solution.py:543

commit v2 on v1

v2 whole, which is shorter than its diff:
```python
import math

import jax
import jax.numpy as jnp
import numpy as np
from jax import lax
from jax.experimental import pallas as pl
from jax.experimental.pallas import tpu as pltpu
from jax.sharding import PartitionSpec as P

MESH = pl.DeviceIdType.MESH
BF16 = jnp.bfloat16
F32 = jnp.float32
NG = 192
SLAB = 24
EXT = 32
COEFFS = (-205.0 / 72.0, 8.0 / 5.0, -1.0 / 5.0, 8.0 / 315.0, -1.0 / 560.0)
WEIGHTS = (8064.0, -1008.0, 128.0, -9.0)
ROWS = 288
PIECE = 4 * ROWS // 8


def cas(product):
    angles = (np.asarray(product, np.int64) % NG).astype(np.float64) * (2.0 * math.pi / NG)
    return np.cos(angles) + np.sin(angles)


def halves(table):
    table = np.asarray(table, np.float32)
    high = table.astype(jnp.bfloat16)
    low = (table - high.astype(np.float32)).astype(jnp.bfloat16)
    return np.stack([high, low])


def tables():
    index = np.arange(NG)
    plain = cas(index[:, None] * index[None, :])
    stencil = np.zeros((NG, NG), np.float32)
    for offset, weight in enumerate(WEIGHTS, 1):
        for sign in (1, -1):
            stencil[index, (index + sign * offset) % NG] += weight
    forward_y = np.zeros((2, 256, 256))
    for layer in range(2):
        forward_y[layer, :128, :NG] = plain[:128]
        forward_y[layer, 128 + 64 * layer : 192 + 64 * layer, :NG] = plain[128:]
    forward_x = np.zeros((NG, 256))
    for core in range(2):
        for space in range(8):
            for slot in range(16):
                step, layer = divmod(slot, 2)
                ext = (14 - 2 * step if core == 0 else 16 + 2 * step) + layer
                x = (SLAB * space + ext - 4) % NG
                forward_x[:, (core * 8 + space) * 16 + slot] = plain[:, x]
    inverse_y = np.zeros((256, 256))
    inverse_z = np.zeros((256, NG))
    for band in range(16):
        inverse_y[band * 16 : band * 16 + 12, :NG] = plain[band * 12 : band * 12 + 12]
        x_lo, y, core = band // 8, (band // 2) % 4, band % 2
        first = 24 * (2 * y + x_lo) + 12 * core
        inverse_z[band * 16 : band * 16 + 12] = plain[first : first + 12]
    pieces = {
        "stencil": stencil.astype(jnp.bfloat16)[None],
        "plain": halves(plain),
        "forward_y0": halves(forward_y[0]),
        "forward_y1": halves(forward_y[1]),
        "forward_x": halves(forward_x),
        "inverse_y": halves(inverse_y),
        "inverse_z": halves(inverse_z),
    }
    where, rows, start = {}, [], 0
    for name, piece in pieces.items():
        count, height, width = piece.shape
        where[name] = (start, count, height, width)
        flat = piece.reshape(count * height, width)
        rows.append(np.pad(flat, ((0, 0), (0, 256 - width))))
        start += count * height
    return where, np.concatenate(rows)


WHERE, TABLE = tables()


def split(value):
    high = value.astype(BF16)
    low = (value - high.astype(F32)).astype(BF16)
    return high, low


def dot(a, b, dims=((1,), (0,))):
    return lax.dot_general(a, b, (dims, ((), ())), preferred_element_type=F32)


def dot3_table_left(table, value, dims=((1,), (0,))):
    high, low = split(value)
    return dot(table[0], high, dims) + (dot(table[1], high, dims) + dot(table[0], low, dims))


def dot3_table_right(value, table):
    high, low = split(value)
    return dot(high, table[0]) + (dot(low, table[0]) + dot(high, table[1]))


def pack_into(ref, index, layer):
    ref[index, :NG, :] = layer[:, :128]
    ref[index, NG:, :64] = layer[:96, 128:]
    ref[index, NG:, 64:] = layer[96:, 128:]


def unpacked(ref, row):
    main = ref[pl.ds(row, NG), :]
    tail = ref[pl.ds(row + NG, 96), :]
    return main, tail


def kernel(
    occ_ref, shift_ref, orb_hbm, pert_hbm, pot_hbm, table_hbm, out,
    table, orb, pert, pot, v, e,
    osend, orecv, psend, precv,
    mine, other, crecv, tiles, ya_recv, xsum, xb_recv, xa_recv, ysum, yb_recv, red,
    gsend, grecv, wsend, wrecv, brow, zsend, zrecv, mat,
    load_sem, osem, psem, fsem, csem, ya_sem, xb_sem, xa_sem, yb_sem, gsem, wsem, zsem, sent,
):
    band = lax.axis_index("band")
    space = lax.axis_index("space")
    core = lax.rem(band, 2)
    y = lax.rem(band // 2, 4)
    x_lo = band // 8
    group = 2 * y + x_lo
    up = lax.rem(space + 1, 8)
    down = lax.rem(space + 7, 8)

    def band_of(x, yy, c):
        return x * 8 + yy * 2 + c

    def y_at(k):
        return lax.rem(y + k, 4)

    def part(name, number=0):
        start, _, height, width = WHERE[name]
        return table[start + number * height : start + (number + 1) * height, :width]

    def pair_of(name):
        return part(name, 0), part(name, 1)

    def wait_bytes(ref, sem):
        pltpu.make_async_copy(ref, ref, sem).wait()

    def send(src, dst, send_sem, recv_sem, to_band, to_space):
        pltpu.make_async_remote_copy(
            src_ref=src,
            dst_ref=dst,
            send_sem=send_sem,
            recv_sem=recv_sem,
            device_id=(to_band, to_space),
            device_id_type=MESH,
        ).start()

    loads = []
    for number, (source, target) in enumerate(
        (
            (pert_hbm.at[0, 0:4], pert.at[4:8]),
            (pert_hbm.at[0, 20:24], pert.at[24:28]),
            (orb_hbm.at[0, 0:4], orb.at[4:8]),
            (orb_hbm.at[0, 20:24], orb.at[24:28]),
            (orb_hbm.at[0, 4:20], orb.at[8:24]),
            (pert_hbm.at[0, 4:20], pert.at[8:24]),
            (pot_hbm, pot),
            (table_hbm, table),
        )
    ):
        copy = pltpu.make_async_copy(source, target, load_sem.at[number])
        copy.start()
        loads.append(copy)

    barrier = pltpu.get_barrier_semaphore()
    for k in range(1, 8):
        for c in range(2):
            pl.semaphore_signal(
                barrier,
                inc=1,
                device_id=(band_of(x_lo, y, c), lax.rem(space + k, 8)),
                device_id_type=MESH,
            )
    for k in range(1, 16):
        pl.semaphore_signal(
            barrier, inc=1, device_id=(lax.rem(band + k, 16), space), device_id_type=MESH
        )

    for layer in list(range(0, 8)) + list(range(32, 40)):
        e[layer] = jnp.zeros((NG, NG), F32)

    delta = 5.5
    shift = jnp.full((1, NG), shift_ref[0], F32)
    theta = shift + 5.5
    ratio = theta / delta
    w0 = 1.0 / ratio
    w1 = 1.0 / (2.0 * ratio - w0)
    w2 = 1.0 / (2.0 * ratio - w1)
    beta1, beta = 2.0 * w1 / delta, 2.0 * w2 / delta
    a_own = w1 * w0 / theta + beta1
    b_own = beta1 / theta
    b_sten = b_own / 10080.0
    q_shift = shift - 1.5 * COEFFS[0]
    g0 = (1.0 - w2 * w0) / theta
    g1 = 1.0 + w2 * w1 + beta / beta1
    beta_sten = beta / 10080.0
    factor = jnp.full((1, NG), occ_ref[0], F32) * (-4.0 / 16.0)

    piece = 4 * core + y
    piece_row = pl.multiple_of(piece * PIECE, 8)
    half_row = pl.multiple_of(lax.rem(piece, 2) * PIECE, 8)
    loads[0].wait()
    loads[1].wait()
    pack_into(psend, 0, pert[24 + piece // 2])
    pack_into(psend, 1, pert[4 + piece // 2])
    loads[2].wait()
    loads[3].wait()

    pl.semaphore_wait(barrier, 29)

    for way, target in ((0, up), (1, down)):
        send(
            psend.at[way, pl.ds(half_row, PIECE)],
            precv.at[way, pl.ds(piece_row, PIECE)],
            sent.at[0], psem.at[way], band, target,
        )
    for near in range(2):
        for way, target in ((0, up), (1, down)):
            first = 2 - 2 * near if way == 0 else 2 * near
            for layer in (first, first + 1):
                pack_into(
                    osend.at[way], layer, orb[(24 if way == 0 else 4) + layer].astype(F32)
                )
            send(
                osend.at[way, first : first + 2],
                orecv.at[way, first : first + 2],
                sent.at[1], osem.at[way, near], band, target,
            )

    loads[4].wait()
    loads[5].wait()

    def make_v(layer, carry):
        v[layer] = orb[layer].astype(F32) * pert[layer]
        return carry

    lax.fori_loop(4, 28, make_v, 0)
    loads[6].wait()
    loads[7].wait()

    def along_x(ref, layer):
        total = WEIGHTS[0] * (ref[layer - 1] + ref[layer + 1])
        for offset in range(2, 5):
            total += WEIGHTS[offset - 1] * (ref[layer - offset] + ref[layer + offset])
        return total

    def shifted(ref, layer):
        value = ref[layer]
        high, low = split(value)
        total = along_x(ref, layer)
        stencil = part("stencil")
        total += dot(high, stencil) + dot(low, stencil)
        total += dot(stencil, high) + dot(stencil, low)
        return value, total

    def make_e(layer, carry):
        value, total = shifted(v, layer + 4)
        diagonal = pot[layer] + q_shift
        e[layer + 8] = (a_own - b_own * diagonal) * value + b_sten * total
        return carry

    def density_own(layer):
        value, total = shifted(e, layer + 4)
        diagonal = pot[layer - 4] + q_shift
        solved = g0 * v[layer] + (g1 - beta * diagonal) * value + beta_sten * total
        return factor * orb[layer].astype(F32) * solved

    def density_beyond(layer):
        return factor * orb[layer].astype(F32) * (beta_sten * along_x(e, layer + 4))

    def base_of(c, j):
        return jnp.where(c == 0, 14 - 2 * j, 16 + 2 * j)

    def make_pairs(j, density):
        def fill(layer, carry):
            other[j, layer] = density(base_of(1 - core, j) + layer)
            return carry

        lax.fori_loop(0, 2, fill, 0)
        send(
            other.at[j], crecv.at[j], sent.at[2], csem.at[j], band_of(x_lo, y, 1 - core), space
        )

        def fill_mine(layer, carry):
            mine[j, layer] = density(base_of(core, j) + layer)
            return carry

        lax.fori_loop(0, 2, fill_mine, 0)

    def transformed(value):
        high, low = split(value)
        last = ((1,), (1,))
        table_high, table_low = pair_of("plain")
        rows = dot(table_high, high, last) + (
            dot(table_low, high, last) + dot(table_high, low, last)
        )
        return rows.reshape(4, 2, 24, NG)

    def add_cores(j):
        wait_bytes(crecv.at[j], csem.at[j])
        first = transformed(mine[j, 0] + crecv[j, 0])
        tiles[j, 0] = first[..., :128]
        tiles[j, 2, :, :, :, :64] = first[..., 128:]
        second = transformed(mine[j, 1] + crecv[j, 1])
        tiles[j, 1] = second[..., :128]
        tiles[j, 2, :, :, :, 64:] = second[..., 128:]

    def ya_start(j):
        add_cores(j)
        for k in (2, 1, 3):
            send(
                tiles.at[j, :, y_at(k)], ya_recv.at[j, k - 1],
                sent.at[3], ya_sem.at[j], band_of(x_lo, y_at(k), core), space,
            )

    def ya_end(j):
        wait_bytes(ya_recv.at[j], ya_sem.at[j])
        xsum[j] = (tiles[j, :, y] + ya_recv[j, 0]) + (ya_recv[j, 1] + ya_recv[j, 2])
        send(
            xsum.at[j, :, 1 - x_lo], xb_recv.at[j],
            sent.at[4], xb_sem.at[j], band_of(1 - x_lo, y, core), space,
        )

    def xb_end(j):
        wait_bytes(xb_recv.at[j], xb_sem.at[j])
        red[j] = xsum[j, :, x_lo] + xb_recv[j]

    def xa_start(j):
        add_cores(j)
        send(
            tiles.at[j, :, :, 1 - x_lo], xa_recv.at[j - 4],
            sent.at[5], xa_sem.at[j - 4], band_of(1 - x_lo, y, core), space,
        )

    def xa_end(j):
        wait_bytes(xa_recv.at[j - 4], xa_sem.at[j - 4])
        ysum[j - 4] = tiles[j, :, :, x_lo] + xa_recv[j - 4]
        for k in (2, 1, 3):
            send(
                ysum.at[j - 4, :, y_at(k)], yb_recv.at[j - 4, k - 1],
                sent.at[6], yb_sem.at[j - 4], band_of(x_lo, y_at(k), core), space,
            )

    def yb_end(j):
        wait_bytes(yb_recv.at[j - 4], yb_sem.at[j - 4])
        red[j] = (ysum[j - 4, :, y] + yb_recv[j - 4, 0]) + (
            yb_recv[j - 4, 1] + yb_recv[j - 4, 2]
        )

    def repeat(lo, hi, *steps):
        def body(j, carry):
            for one in steps:
                one(j)
            return carry

        lax.fori_loop(lo, hi, body, 0)

    lax.fori_loop(4, 12, make_e, 0)

    for way in range(2):
        wait_bytes(precv.at[way, :PIECE], psem.at[way])
    for way in range(2):
        for k in (2, 1, 3):
            send(
                precv.at[way, pl.ds(piece_row, PIECE)],
                precv.at[way, pl.ds(piece_row, PIECE)],
                sent.at[7], fsem.at[0], band_of(x_lo, y_at(k), core), space,
            )
    lax.fori_loop(12, 20, make_e, 0)
    repeat(0, 1, lambda j: make_pairs(j, density_own))
    wait_bytes(precv.at[0, : 6 * PIECE], fsem.at[0])
    core_row = pl.multiple_of(core * 4 * PIECE, 8)
    for way in range(2):
        send(
            precv.at[way, pl.ds(core_row, 4 * PIECE)],
            precv.at[way, pl.ds(core_row, 4 * PIECE)],
            sent.at[8], fsem.at[1], band_of(x_lo, y, 1 - core), space,
        )
    repeat(1, 2, lambda j: make_pairs(j, density_own))
    repeat(0, 2, ya_start)

    def take_halo(near):
        for way in range(2):
            first = 2 - 2 * near if way == 0 else 2 * near
            wait_bytes(orecv.at[way, first : first + 2], osem.at[way, near])
            for layer in (first, first + 1):
                at = layer + (0 if way == 0 else 28)
                main, tail = unpacked(orecv.at[way, layer], 0)
                pmain, ptail = unpacked(precv.at[way], layer * ROWS)
                orb[at, :, :128] = main.astype(BF16)
                orb[at, :96, 128:] = tail[:, :64].astype(BF16)
                orb[at, 96:, 128:] = tail[:, 64:].astype(BF16)
                main = main * pmain
                tail = tail * ptail
                v[at, :, :128] = main
                v[at, :96, 128:] = tail[:, :64]
                v[at, 96:, 128:] = tail[:, 64:]
        repeat(2 - 2 * near, 4 - 2 * near, lambda j: make_e(j, 0))
        repeat(20 + 2 * near, 22 + 2 * near, lambda j: make_e(j, 0))

    wait_bytes(precv.at[0, : 8 * PIECE], fsem.at[1])
    take_halo(0)
    repeat(2, 3, lambda j: make_pairs(j, density_own), ya_start)
    repeat(0, 3, ya_end)
    take_halo(1)
    repeat(3, 5, lambda j: make_pairs(j, density_own))
    repeat(3, 4, ya_start)

    def tail(j):
        @pl.when(j < 5)
        def _():
            make_pairs(j + 1, density_own)

        @pl.when(jnp.logical_and(j >= 5, j < 7))
        def _():
            make_pairs(j + 1, density_beyond)

        xa_start(j)

        @pl.when(j >= 6)
        def _():
            xa_end(j - 2)

    repeat(4, 8, tail)
    repeat(3, 4, ya_end)
    repeat(6, 8, xa_end)
    repeat(0, 4, xb_end)
    repeat(4, 8, yb_end)

    red0 = jnp.concatenate([red[:, 0].reshape(NG, 128), red[:, 2].reshape(NG, 128)], axis=1)
    red1 = jnp.concatenate([red[:, 1].reshape(NG, 128), red[:, 2].reshape(NG, 128)], axis=1)
    for layer, value in enumerate((red0, red1)):
        high, low = split(value)
        table_high, table_low = pair_of("forward_y%d" % layer)
        columns = dot(high, table_high) + (dot(low, table_high) + dot(high, table_low))
        for j in range(8):
            for half in range(2):
                gsend[pl.ds(half * 16 + 2 * j + layer, 24, stride=32), :] = columns[
                    24 * j : 24 * j + 24, 128 * half : 128 * half + 128
                ]

    mine_at = core * 8 + space

    for k in (4, 3, 5, 2, 6, 1, 7, 0):
        for c in range(2):
            if (k, c) != (0, 0):
                to_space = lax.rem(space + k, 8)
                to_core = lax.rem(core + c, 2)
                row = pl.multiple_of(48 * (to_core * 8 + to_space), 8)
                send(
                    gsend.at[pl.ds(row, 48)], grecv.at[mine_at],
                    gsem.at[0], gsem.at[1], band_of(x_lo, y, to_core), to_space,
                )
    grecv[mine_at] = gsend[pl.ds(pl.multiple_of(48 * mine_at, 8), 48), :]

    kx = lax.broadcasted_iota(jnp.int32, (NG, 128), 0)
    lane = lax.broadcasted_iota(jnp.int32, (NG, 128), 1)
    gx = jnp.minimum(kx, NG - kx)
    factors = []
    for unit in range(3):
        number = 3 * mine_at + unit
        kz = 24 * group + number // 2
        gz = jnp.minimum(kz, NG - kz)
        ky = lane + 128 * lax.rem(number, 2)
        gy = jnp.minimum(ky, NG - ky)
        square = (gx * gx + gy * gy + (gz * gz + 1)).astype(F32)
        factors.append((256.0 / float(NG) ** 3) / jnp.sqrt(square))
    coulomb = jnp.concatenate(factors, axis=1)

    wait_bytes(grecv.at[:15], gsem.at[1])
    pencil = jnp.concatenate(
        [grecv[:, 16 * unit : 16 * unit + 16, :].reshape(256, 128) for unit in range(3)], axis=1
    )
    spectral = dot3_table_left(pair_of("forward_x"), pencil) * coulomb
    restored = dot3_table_left(pair_of("plain"), spectral)
    for unit in range(3):
        wsend[unit] = restored[:, 128 * unit : 128 * unit + 128]

    for k in (4, 3, 5, 2, 6, 1, 7):
        to_space = lax.rem(space + k, 8)
        row = pl.multiple_of(24 * to_space, 8)
        send(
            wsend.at[:, pl.ds(row, 24)], wrecv.at[pl.ds(3 * space, 3)],
            wsem.at[0], wsem.at[1], band, to_space,
        )
    wrecv[pl.ds(3 * space, 3)] = wsend[:, pl.ds(pl.multiple_of(24 * space, 8), 24), :]
    brow[...] = jnp.zeros(brow.shape, F32)
    wait_bytes(wrecv.at[:21], wsem.at[1])

    for unit in range(24):
        brow[unit % 2, pl.ds(unit // 2, 24, stride=16), :] = wrecv[unit]
    rows = jnp.concatenate([brow[0], brow[1]], axis=1)
    zsend[...] = dot3_table_left(pair_of("inverse_y"), rows, ((1,), (1,)))

    for k in (4, 12, 8, 3, 5, 11, 13, 2, 6, 10, 14, 7, 9, 1, 15):
        to = lax.rem(band + k, 16)
        send(
            zsend.at[pl.ds(pl.multiple_of(16 * to, 8), 16)], zrecv.at[band],
            zsem.at[0], zsem.at[1], to, space,
        )
    zrecv[band] = zsend[pl.ds(pl.multiple_of(16 * band, 8), 16), :]
    wait_bytes(zrecv.at[:15], zsem.at[1])

    granule = lax.broadcasted_iota(jnp.int32, (16, 128), 1) // 16
    for third in range(3):
        for side in range(2):
            blocks = [zrecv[8 * side + i, :, 128 * third : 128 * third + 128] for i in range(8)]
            for bit in (1, 2, 4):
                upper = lax.rem(granule // bit, 2) == 1
                after = list(blocks)
                for i in range(8):
                    if not i & bit:
                        low, high = blocks[i], blocks[i | bit]
                        after[i] = jnp.where(upper, pltpu.roll(high, 16 * bit, 1), low)
                        after[i | bit] = jnp.where(upper, high, pltpu.roll(low, 128 - 16 * bit, 1))
                blocks = after
            for i in range(8):
                x = 8 * third + i
                mat[16 * x : 16 * x + 16, 128 * side : 128 * side + 128] = blocks[i]
    result = dot3_table_right(mat[...], pair_of("inverse_z"))
    for x in range(SLAB):
        out[0, x] = result[16 * x : 16 * x + 12]

    wait_bytes(psend.at[:, :PIECE], sent.at[0])
    wait_bytes(osend, sent.at[1])
    wait_bytes(other, sent.at[2])
    wait_bytes(ya_recv, sent.at[3])
    wait_bytes(xb_recv, sent.at[4])
    wait_bytes(xa_recv, sent.at[5])
    wait_bytes(yb_recv, sent.at[6])
    wait_bytes(precv.at[0, : 6 * PIECE], sent.at[7])
    wait_bytes(precv.at[0, : 8 * PIECE], sent.at[8])
    wait_bytes(grecv.at[:15], gsem.at[0])
    wait_bytes(wrecv.at[:21], wsem.at[0])
    wait_bytes(zrecv.at[:15], zsem.at[0])


def on_device(orbitals, occupations, shifts, perturbations, local_potential):
    any_space = pl.BlockSpec(memory_space=pl.ANY)
    smem = pl.BlockSpec(memory_space=pltpu.SMEM)
    vmem = pl.BlockSpec(memory_space=pltpu.VMEM)
    dma = pltpu.SemaphoreType.DMA
    return pl.pallas_call(
        kernel,
        out_shape=jax.ShapeDtypeStruct((1, SLAB, 12, NG), F32),
        in_specs=[smem] * 2 + [any_space] * 4,
        out_specs=vmem,
        scratch_shapes=[
            pltpu.VMEM(TABLE.shape, BF16),
            pltpu.VMEM((EXT, NG, NG), BF16),
            pltpu.VMEM((EXT, NG, NG), F32),
            pltpu.VMEM((SLAB, NG, NG), F32),
            pltpu.VMEM((EXT, NG, NG), F32),
            pltpu.VMEM((EXT + 8, NG, NG), F32),
            pltpu.VMEM((2, 4, ROWS, 128), F32),
            pltpu.VMEM((2, 4, ROWS, 128), F32),
            pltpu.VMEM((2, ROWS, 128), F32),
            pltpu.VMEM((2, 4 * ROWS, 128), F32),
            pltpu.VMEM((8, 2, NG, NG), F32),
            pltpu.VMEM((8, 2, NG, NG), F32),
            pltpu.VMEM((8, 2, NG, NG), F32),
            pltpu.VMEM((8, 3, 4, 2, 24, 128), F32),
            pltpu.VMEM((4, 3, 3, 2, 24, 128), F32),
            pltpu.VMEM((4, 3, 2, 24, 128), F32),
            pltpu.VMEM((4, 3, 24, 128), F32),
            pltpu.VMEM((4, 3, 4, 24, 128), F32),
            pltpu.VMEM((4, 3, 4, 24, 128), F32),
            pltpu.VMEM((4, 3, 3, 24, 128), F32),
            pltpu.VMEM((8, 3, 24, 128), F32),
            pltpu.VMEM((768, 128), F32),
            pltpu.VMEM((16, 48, 128), F32),
            pltpu.VMEM((3, NG, 128), F32),
            pltpu.VMEM((24, 24, 128), F32),
            pltpu.VMEM((2, 384, 128), F32),
            pltpu.VMEM((256, 384), F32),
            pltpu.VMEM((16, 16, 384), F32),
            pltpu.VMEM((384, 256), F32),
            dma((8,)),
            dma((2, 2)),
            dma((2,)),
            dma((2,)),
            dma((8,)),
            dma((4,)),
            dma((4,)),
            dma((4,)),
            dma((4,)),
            dma((2,)),
            dma((2,)),
            dma((2,)),
            dma((9,)),
        ],
        compiler_params=pltpu.CompilerParams(
            collective_id=0, has_side_effects=True, vmem_limit_bytes=60 * 2**20
        ),
        name="response",
    )(occupations, shifts, orbitals, perturbations, local_potential, jnp.asarray(TABLE))


def solution(mesh):
    in_specs = (
        P("band", "space", None, None),
        P("band"),
        P("band"),
        P(None, "space", None, None),
        P("space", None, None),
    )
    out_specs = P(None, "space", "band", None)
    return jax.shard_map(
        on_device, mesh=mesh, in_specs=in_specs, out_specs=out_specs, check_vma=False
    )
```

time: 101 us -> 89.2 us (0.88)
  Pallas kernels: 96.3 us -> 85.9 us
    pallas_call x1, Pallas kernels: 96.3 us -> 85.9 us  [on_device(): pl.pallas_call(kernel, out_shape=jax.ShapeDtypeStruct((1, SLAB, 12, NG),...]
where the time goes in v2:
time: 89.2 us; the launch traced here: 89.1 us
  Pallas kernels  85.9 us (96%)
  local copies, waits for them, and re-layouts  1.88 us (2%)
  between operations  1.3 us (1%)
    pallas_call x1, Pallas kernels, on_device(): pl.pallas_call(kernel, out_shape=jax.ShapeDtypeStruct((1, SLAB, 12, NG),...  85.9 us
    pallas_call x1, local copies, waits for them, and re-layouts, on_device(): pl.pallas_call(kernel, out_shape=jax.ShapeDtypeStruct((1, SLAB, 12, NG),...  1.88 us

profile of v2, /device:TPU:1, one launch (start us, length us, event | category | flops | bytes accessed | tf_op | source)
XLA Modules:
  0.0 89.1 jit_solution(7741280755421481392)
XLA Ops:
  1.3 85.9 %response.1 = f32[1,24,12,192]{3,2,1,0:T(8,128)} custom-call(f32[1]{0:T(128)S(6)} %copy.8.occ_ref, f32[1]{0:T(128)S(6)} %copy.9.shift_ref, bf16[1,24,192,192]{3,2,1,0:T(8,128)(2,1)} %orb_hbm.1, f32[1,24,192,192]{3,2,1,0:T(8,128)} %pert_hbm.1, f32[24,192,192]{2,1,0:T(8,128)} %pot_hbm.1, bf16[3008,256]{1,0:T(8,128)(2,1)} %constant.2.clone.table_hbm), custom_call_target="tpu_custom_call" | custom-call | tf_op jit(solution)/shard_map/response/pallas_call | solution.py:553
  87.2 1.9 %copy.7 = f32[1,24,12,192]{3,1,2,0:T(8,128)} copy(f32[1,24,12,192]{3,2,1,0:T(8,128)} %response.1) | data formatting | bytes 442368 | tf_op jit(solution)/shard_map/response/pallas_call | solution.py:553

commit v3 on v2

--- a/solution.py
+++ b/solution.py
@@ -18,6 +18,14 @@
 WEIGHTS = (8064.0, -1008.0, 128.0, -9.0)
 ROWS = 288
 PIECE = 4 * ROWS // 8
+CHUNKS = (
+    (0, 80, ((0, 184, 8), (8, 0, 72))),
+    (120, 64, ((0, 72, 64),)),
+    (216, 48, ((0, 136, 48),)),
+)
+ITEMS = ((0, 0), (1, 0), (2, 0), (0, 1), (0, 2), (0, 3), (1, 1), (1, 2), (1, 3), (2, 3), (2, 1), (2, 2))
+X_FIRST = (9, 11)
+Y_FIRST = tuple(n for n in range(12) if n not in X_FIRST)
 
 
 def cas(product):
@@ -39,18 +47,24 @@
     for offset, weight in enumerate(WEIGHTS, 1):
         for sign in (1, -1):
             stencil[index, (index + sign * offset) % NG] += weight
-    forward_y = np.zeros((2, 256, 256))
+    window = np.zeros((64, 80), np.float32)
+    for offset, weight in enumerate(WEIGHTS, 1):
+        for sign in (1, -1):
+            window[np.arange(64), np.arange(64) + 8 + sign * offset] += weight
+    forward_y = np.zeros((2, 384, 256))
     for layer in range(2):
-        forward_y[layer, :128, :NG] = plain[:128]
-        forward_y[layer, 128 + 64 * layer : 192 + 64 * layer, :NG] = plain[128:]
+        for chunk in range(3):
+            first = 128 * chunk + 64 * layer
+            forward_y[layer, first : first + 64, :NG] = plain[64 * chunk : 64 * chunk + 64]
     forward_x = np.zeros((NG, 256))
     for core in range(2):
         for space in range(8):
             for slot in range(16):
-                step, layer = divmod(slot, 2)
-                ext = (14 - 2 * step if core == 0 else 16 + 2 * step) + layer
+                block, layer = divmod(slot, 4)
+                ext = (12 - 4 * block if core == 0 else 16 + 4 * block) + layer
                 x = (SLAB * space + ext - 4) % NG
-                forward_x[:, (core * 8 + space) * 16 + slot] = plain[:, x]
+                column = 128 * (slot // 8) + (core * 8 + space) * 8 + slot % 8
+                forward_x[:, column] = plain[:, x]
     inverse_y = np.zeros((256, 256))
     inverse_z = np.zeros((256, NG))
     for band in range(16):
@@ -60,6 +74,7 @@
         inverse_z[band * 16 : band * 16 + 12] = plain[first : first + 12]
     pieces = {
         "stencil": stencil.astype(jnp.bfloat16)[None],
+        "window": window.astype(jnp.bfloat16)[None],
         "plain": halves(plain),
         "forward_y0": halves(forward_y[0]),
         "forward_y1": halves(forward_y[1]),
@@ -101,21 +116,32 @@
 
 
 def pack_into(ref, index, layer):
-    ref[index, :NG, :] = layer[:, :128]
-    ref[index, NG:, :64] = layer[:96, 128:]
-    ref[index, NG:, 64:] = layer[96:, 128:]
-
-
-def unpacked(ref, row):
-    main = ref[pl.ds(row, NG), :]
-    tail = ref[pl.ds(row + NG, 96), :]
-    return main, tail
+    for start, count, places in CHUNKS:
+        rows = [layer[row : row + size] for _, row, size in places]
+        rows = rows[0] if len(rows) == 1 else jnp.concatenate(rows, axis=0)
+        half = count // 2
+        ref[index, start : start + count, :] = rows[:, :128]
+        ref[index, start + count : start + count + half, :64] = rows[:half, 128:]
+        ref[index, start + count : start + count + half, 64:] = rows[half:, 128:]
+
+
+def unpack_into(ref, where, chunk, main, tail):
+    _, count, places = CHUNKS[chunk]
+    half = count // 2
+    for at, row, size in places:
+        ref[*where, row : row + size, :128] = main[at : at + size]
+        for lo, hi, lane in ((0, half, 0), (half, count, 64)):
+            first, last = max(at, lo), min(at + size, hi)
+            if first < last:
+                ref[*where, row + first - at : row + last - at, 128:] = tail[
+                    first - lo : last - lo, lane : lane + 64
+                ]
 
 
 def kernel(
     occ_ref, shift_ref, orb_hbm, pert_hbm, pot_hbm, table_hbm, out,
     table, orb, pert, pot, v, e,
-    osend, orecv, psend, precv,
+    osend, orecv, psend, precv, orb_halo, v_halo,
     mine, other, crecv, tiles, ya_recv, xsum, xb_recv, xa_recv, ysum, yb_recv, red,
     gsend, grecv, wsend, wrecv, brow, zsend, zrecv, mat,
     load_sem, osem, psem, fsem, csem, ya_sem, xb_sem, xa_sem, yb_sem, gsem, wsem, zsem, sent,
@@ -188,6 +214,8 @@
 
     for layer in list(range(0, 8)) + list(range(32, 40)):
         e[layer] = jnp.zeros((NG, NG), F32)
+    for layer in (0, 1, 2, 3, 28, 29, 30, 31):
+        v[layer] = jnp.zeros((NG, NG), F32)
 
     delta = 5.5
     shift = jnp.full((1, NG), shift_ref[0], F32)
@@ -224,17 +252,15 @@
             precv.at[way, pl.ds(piece_row, PIECE)],
             sent.at[0], psem.at[way], band, target,
         )
-    for near in range(2):
+    for way in range(2):
+        for layer in range(4):
+            pack_into(osend.at[way], layer, orb[(24 if way == 0 else 4) + layer].astype(F32))
+    for chunk, (start, count, _) in enumerate(CHUNKS):
         for way, target in ((0, up), (1, down)):
-            first = 2 - 2 * near if way == 0 else 2 * near
-            for layer in (first, first + 1):
-                pack_into(
-                    osend.at[way], layer, orb[(24 if way == 0 else 4) + layer].astype(F32)
-                )
             send(
-                osend.at[way, first : first + 2],
-                orecv.at[way, first : first + 2],
-                sent.at[1], osem.at[way, near], band, target,
+                osend.at[way, :, start : start + 3 * count // 2],
+                orecv.at[way, :, start : start + 3 * count // 2],
+                sent.at[1], osem.at[way, chunk], band, target,
             )
 
     loads[4].wait()
@@ -248,122 +274,122 @@
     loads[6].wait()
     loads[7].wait()
 
-    def along_x(ref, layer):
-        total = WEIGHTS[0] * (ref[layer - 1] + ref[layer + 1])
+    def along_x(ref, layer, rows):
+        total = WEIGHTS[0] * (ref[layer - 1, rows] + ref[layer + 1, rows])
         for offset in range(2, 5):
-            total += WEIGHTS[offset - 1] * (ref[layer - offset] + ref[layer + offset])
+            total += WEIGHTS[offset - 1] * (
+                ref[layer - offset, rows] + ref[layer + offset, rows]
+            )
         return total
 
-    def shifted(ref, layer):
-        value = ref[layer]
+    def make_e(layer, carry):
+        value = v[layer + 4]
         high, low = split(value)
-        total = along_x(ref, layer)
         stencil = part("stencil")
+        total = along_x(v, layer + 4, slice(None))
         total += dot(high, stencil) + dot(low, stencil)
         total += dot(stencil, high) + dot(stencil, low)
-        return value, total
-
-    def make_e(layer, carry):
-        value, total = shifted(v, layer + 4)
         diagonal = pot[layer] + q_shift
         e[layer + 8] = (a_own - b_own * diagonal) * value + b_sten * total
         return carry
 
-    def density_own(layer):
-        value, total = shifted(e, layer + 4)
-        diagonal = pot[layer - 4] + q_shift
-        solved = g0 * v[layer] + (g1 - beta * diagonal) * value + beta_sten * total
-        return factor * orb[layer].astype(F32) * solved
-
-    def density_beyond(layer):
-        return factor * orb[layer].astype(F32) * (beta_sten * along_x(e, layer + 4))
-
-    def base_of(c, j):
-        return jnp.where(c == 0, 14 - 2 * j, 16 + 2 * j)
-
-    def make_pairs(j, density):
-        def fill(layer, carry):
-            other[j, layer] = density(base_of(1 - core, j) + layer)
-            return carry
-
-        lax.fori_loop(0, 2, fill, 0)
+    def density_own(layer, chunk):
+        rows = slice(64 * chunk, 64 * chunk + 64)
+        around = {0: ((184, 192), (0, 72)), 1: ((56, 136),), 2: ((120, 192), (0, 8))}[chunk]
+        pieces = [e[layer + 4, lo:hi] for lo, hi in around]
+        high, low = split(pieces[0] if len(pieces) == 1 else jnp.concatenate(pieces, axis=0))
+        window = part("window")
+        total = along_x(e, layer + 4, rows) + (dot(window, high) + dot(window, low))
+        value = e[layer + 4, rows]
+        high, low = split(value)
+        stencil = part("stencil")
+        total += dot(high, stencil) + dot(low, stencil)
+        diagonal = pot[layer - 4, rows] + q_shift
+        solved = g0 * v[layer, rows] + (g1 - beta * diagonal) * value + beta_sten * total
+        return factor * orb[layer, rows].astype(F32) * solved
+
+    def density_beyond(layer, chunk):
+        rows = slice(64 * chunk, 64 * chunk + 64)
+        at = jnp.where(layer < 4, layer, layer - 24)
+        return factor * orb_halo[at, rows] * (beta_sten * along_x(e, layer + 4, rows))
+
+    def make_item(n):
+        chunk, block = ITEMS[n]
+        density = density_beyond if block == 3 else density_own
+
+        def fill(ref, c):
+            base = jnp.where(c == 0, 12 - 4 * block, 16 + 4 * block)
+
+            def body(layer, carry):
+                ref[n, layer] = density(base + layer, chunk)
+                return carry
+
+            lax.fori_loop(0, 4, body, 0)
+
+        fill(other, 1 - core)
         send(
-            other.at[j], crecv.at[j], sent.at[2], csem.at[j], band_of(x_lo, y, 1 - core), space
-        )
-
-        def fill_mine(layer, carry):
-            mine[j, layer] = density(base_of(core, j) + layer)
-            return carry
-
-        lax.fori_loop(0, 2, fill_mine, 0)
-
-    def transformed(value):
-        high, low = split(value)
+            other.at[n], crecv.at[n], sent.at[2], csem.at[n], band_of(x_lo, y, 1 - core), space
+        )
+        fill(mine, core)
+
+    def add_cores(n):
+        wait_bytes(crecv.at[n], csem.at[n])
+        high, low = split((mine[n] + crecv[n]).reshape(256, NG))
+        table_high, table_low = pair_of("plain")
         last = ((1,), (1,))
-        table_high, table_low = pair_of("plain")
         rows = dot(table_high, high, last) + (
             dot(table_low, high, last) + dot(table_high, low, last)
         )
-        return rows.reshape(4, 2, 24, NG)
-
-    def add_cores(j):
-        wait_bytes(crecv.at[j], csem.at[j])
-        first = transformed(mine[j, 0] + crecv[j, 0])
-        tiles[j, 0] = first[..., :128]
-        tiles[j, 2, :, :, :, :64] = first[..., 128:]
-        second = transformed(mine[j, 1] + crecv[j, 1])
-        tiles[j, 1] = second[..., :128]
-        tiles[j, 2, :, :, :, 64:] = second[..., 128:]
-
-    def ya_start(j):
-        add_cores(j)
+        for slot in range(2):
+            tiles[n, slot] = rows[:, 128 * slot : 128 * slot + 128].reshape(4, 2, 24, 128)
+
+    def ya_start(n):
+        add_cores(n)
+        i = Y_FIRST.index(n)
         for k in (2, 1, 3):
             send(
-                tiles.at[j, :, y_at(k)], ya_recv.at[j, k - 1],
-                sent.at[3], ya_sem.at[j], band_of(x_lo, y_at(k), core), space,
+                tiles.at[n, :, y_at(k)], ya_recv.at[i, k - 1],
+                sent.at[3], ya_sem.at[i], band_of(x_lo, y_at(k), core), space,
             )
 
-    def ya_end(j):
-        wait_bytes(ya_recv.at[j], ya_sem.at[j])
-        xsum[j] = (tiles[j, :, y] + ya_recv[j, 0]) + (ya_recv[j, 1] + ya_recv[j, 2])
+    def ya_end(n):
+        i = Y_FIRST.index(n)
+        wait_bytes(ya_recv.at[i], ya_sem.at[i])
+        xsum[i] = (tiles[n, :, y] + ya_recv[i, 0]) + (ya_recv[i, 1] + ya_recv[i, 2])
         send(
-            xsum.at[j, :, 1 - x_lo], xb_recv.at[j],
-            sent.at[4], xb_sem.at[j], band_of(1 - x_lo, y, core), space,
-        )
-
-    def xb_end(j):
-        wait_bytes(xb_recv.at[j], xb_sem.at[j])
-        red[j] = xsum[j, :, x_lo] + xb_recv[j]
-
-    def xa_start(j):
-        add_cores(j)
+            xsum.at[i, :, 1 - x_lo], xb_recv.at[i],
+            sent.at[4], xb_sem.at[i], band_of(1 - x_lo, y, core), space,
+        )
+
+    def xb_end(n):
+        i = Y_FIRST.index(n)
+        chunk, block = ITEMS[n]
+        wait_bytes(xb_recv.at[i], xb_sem.at[i])
+        red[chunk, block] = xsum[i, :, x_lo] + xb_recv[i]
+
+    def xa_start(n):
+        add_cores(n)
+        i = X_FIRST.index(n)
         send(
-            tiles.at[j, :, :, 1 - x_lo], xa_recv.at[j - 4],
-            sent.at[5], xa_sem.at[j - 4], band_of(1 - x_lo, y, core), space,
-        )
-
-    def xa_end(j):
-        wait_bytes(xa_recv.at[j - 4], xa_sem.at[j - 4])
-        ysum[j - 4] = tiles[j, :, :, x_lo] + xa_recv[j - 4]
+            tiles.at[n, :, :, 1 - x_lo], xa_recv.at[i],
+            sent.at[5], xa_sem.at[i], band_of(1 - x_lo, y, core), space,
+        )
+
+    def xa_end(n):
+        i = X_FIRST.index(n)
+        wait_bytes(xa_recv.at[i], xa_sem.at[i])
+        ysum[i] = tiles[n, :, :, x_lo] + xa_recv[i]
         for k in (2, 1, 3):
             send(
-                ysum.at[j - 4, :, y_at(k)], yb_recv.at[j - 4, k - 1],
-                sent.at[6], yb_sem.at[j - 4], band_of(x_lo, y_at(k), core), space,
+                ysum.at[i, :, y_at(k)], yb_recv.at[i, k - 1],
+                sent.at[6], yb_sem.at[i], band_of(x_lo, y_at(k), core), space,
             )
 
-    def yb_end(j):
-        wait_bytes(yb_recv.at[j - 4], yb_sem.at[j - 4])
-        red[j] = (ysum[j - 4, :, y] + yb_recv[j - 4, 0]) + (
-            yb_recv[j - 4, 1] + yb_recv[j - 4, 2]
-        )
-
-    def repeat(lo, hi, *steps):
-        def body(j, carry):
-            for one in steps:
-                one(j)
-            return carry
-
-        lax.fori_loop(lo, hi, body, 0)
+    def yb_end(n):
+        i = X_FIRST.index(n)
+        chunk, block = ITEMS[n]
+        wait_bytes(yb_recv.at[i], yb_sem.at[i])
+        red[chunk, block] = (ysum[i, :, y] + yb_recv[i, 0]) + (yb_recv[i, 1] + yb_recv[i, 2])
 
     lax.fori_loop(4, 12, make_e, 0)
 
@@ -377,7 +403,7 @@
                 sent.at[7], fsem.at[0], band_of(x_lo, y_at(k), core), space,
             )
     lax.fori_loop(12, 20, make_e, 0)
-    repeat(0, 1, lambda j: make_pairs(j, density_own))
+    make_item(0)
     wait_bytes(precv.at[0, : 6 * PIECE], fsem.at[0])
     core_row = pl.multiple_of(core * 4 * PIECE, 8)
     for way in range(2):
@@ -386,82 +412,107 @@
             precv.at[way, pl.ds(core_row, 4 * PIECE)],
             sent.at[8], fsem.at[1], band_of(x_lo, y, 1 - core), space,
         )
-    repeat(1, 2, lambda j: make_pairs(j, density_own))
-    repeat(0, 2, ya_start)
-
-    def take_halo(near):
+    make_item(1)
+    ya_start(0)
+    make_item(2)
+    ya_start(1)
+    lax.fori_loop(0, 4, make_e, 0)
+    ya_start(2)
+    lax.fori_loop(20, 24, make_e, 0)
+
+    def take_halo(chunk):
+        start, count, places = CHUNKS[chunk]
+        half = count // 2
         for way in range(2):
-            first = 2 - 2 * near if way == 0 else 2 * near
-            wait_bytes(orecv.at[way, first : first + 2], osem.at[way, near])
-            for layer in (first, first + 1):
-                at = layer + (0 if way == 0 else 28)
-                main, tail = unpacked(orecv.at[way, layer], 0)
-                pmain, ptail = unpacked(precv.at[way], layer * ROWS)
-                orb[at, :, :128] = main.astype(BF16)
-                orb[at, :96, 128:] = tail[:, :64].astype(BF16)
-                orb[at, 96:, 128:] = tail[:, 64:].astype(BF16)
-                main = main * pmain
-                tail = tail * ptail
-                v[at, :, :128] = main
-                v[at, :96, 128:] = tail[:, :64]
-                v[at, 96:, 128:] = tail[:, 64:]
-        repeat(2 - 2 * near, 4 - 2 * near, lambda j: make_e(j, 0))
-        repeat(20 + 2 * near, 22 + 2 * near, lambda j: make_e(j, 0))
+            wait_bytes(orecv.at[way, :, start : start + count + half], osem.at[way, chunk])
+            for layer in range(4):
+                main = orecv[way, layer, start : start + count]
+                tail = orecv[way, layer, start + count : start + count + half]
+                row = layer * ROWS + start
+                unpack_into(orb_halo, (4 * way + layer,), chunk, main, tail)
+                main = main * precv[way, row : row + count]
+                tail = tail * precv[way, row + count : row + count + half]
+                unpack_into(v_halo, (4 * way + layer,), chunk, main, tail)
+        for _, row, size in places:
+            rows = slice(row, row + size)
+            for x in range(4):
+                below = WEIGHTS[3] * v_halo[x, rows]
+                for layer in range(x + 1, 4):
+                    below += WEIGHTS[3 + x - layer] * v_halo[layer, rows]
+                e[x + 8, rows] += b_sten * below
+                above = WEIGHTS[3] * v_halo[4 + x, rows]
+                for layer in range(x):
+                    above += WEIGHTS[3 + layer - x] * v_halo[4 + layer, rows]
+                e[x + 28, rows] += b_sten * above
 
     wait_bytes(precv.at[0, : 8 * PIECE], fsem.at[1])
     take_halo(0)
-    repeat(2, 3, lambda j: make_pairs(j, density_own), ya_start)
-    repeat(0, 3, ya_end)
+    make_item(3)
+    make_item(4)
+    ya_start(3)
+    make_item(5)
+    ya_start(4)
+    ya_start(5)
+    for n in range(0, 3):
+        ya_end(n)
     take_halo(1)
-    repeat(3, 5, lambda j: make_pairs(j, density_own))
-    repeat(3, 4, ya_start)
-
-    def tail(j):
-        @pl.when(j < 5)
-        def _():
-            make_pairs(j + 1, density_own)
-
-        @pl.when(jnp.logical_and(j >= 5, j < 7))
-        def _():
-            make_pairs(j + 1, density_beyond)
-
-        xa_start(j)
-
-        @pl.when(j >= 6)
-        def _():
-            xa_end(j - 2)
-
-    repeat(4, 8, tail)
-    repeat(3, 4, ya_end)
-    repeat(6, 8, xa_end)
-    repeat(0, 4, xb_end)
-    repeat(4, 8, yb_end)
-
-    red0 = jnp.concatenate([red[:, 0].reshape(NG, 128), red[:, 2].reshape(NG, 128)], axis=1)
-    red1 = jnp.concatenate([red[:, 1].reshape(NG, 128), red[:, 2].reshape(NG, 128)], axis=1)
-    for layer, value in enumerate((red0, red1)):
+    make_item(6)
+    make_item(7)
+    ya_start(6)
+    make_item(8)
+    ya_start(7)
+    ya_start(8)
+    for n in range(3, 6):
+        ya_end(n)
+    take_halo(2)
+    make_item(9)
+    make_item(10)
+    xa_start(9)
+    make_item(11)
+    ya_start(10)
+    xa_start(11)
+    for n in range(6, 9):
+        ya_end(n)
+    xa_end(9)
+    for n in range(0, 6):
+        xb_end(n)
+
+    mine_at = core * 8 + space
+
+    def to_columns(side):
+        blocks = slice(2 * side, 2 * side + 2)
+        value = jnp.concatenate(
+            [red[chunk, blocks].reshape(96, 128) for chunk in range(3)], axis=1
+        )
         high, low = split(value)
-        table_high, table_low = pair_of("forward_y%d" % layer)
-        columns = dot(high, table_high) + (dot(low, table_high) + dot(high, table_low))
-        for j in range(8):
-            for half in range(2):
-                gsend[pl.ds(half * 16 + 2 * j + layer, 24, stride=32), :] = columns[
-                    24 * j : 24 * j + 24, 128 * half : 128 * half + 128
-                ]
-
-    mine_at = core * 8 + space
-
-    for k in (4, 3, 5, 2, 6, 1, 7, 0):
-        for c in range(2):
-            if (k, c) != (0, 0):
-                to_space = lax.rem(space + k, 8)
-                to_core = lax.rem(core + c, 2)
-                row = pl.multiple_of(48 * (to_core * 8 + to_space), 8)
-                send(
-                    gsend.at[pl.ds(row, 48)], grecv.at[mine_at],
-                    gsem.at[0], gsem.at[1], band_of(x_lo, y, to_core), to_space,
-                )
-    grecv[mine_at] = gsend[pl.ds(pl.multiple_of(48 * mine_at, 8), 48), :]
+        for layer in range(2):
+            table_high, table_low = pair_of("forward_y%d" % layer)
+            columns = dot(high, table_high) + (dot(low, table_high) + dot(high, table_low))
+            for j in range(4):
+                for half in range(2):
+                    gsend[side, pl.ds(half * 8 + 2 * j + layer, 24, stride=16), :] = columns[
+                        24 * j : 24 * j + 24, 128 * half : 128 * half + 128
+                    ]
+        for k in (4, 3, 5, 2, 6, 1, 7, 0):
+            for c in range(2):
+                if (k, c) != (0, 0):
+                    to_space = lax.rem(space + k, 8)
+                    to_core = lax.rem(core + c, 2)
+                    row = pl.multiple_of(24 * (to_core * 8 + to_space), 8)
+                    send(
+                        gsend.at[side, pl.ds(row, 24)], grecv.at[side, mine_at],
+                        gsem.at[2], gsem.at[side], band_of(x_lo, y, to_core), to_space,
+                    )
+        grecv[side, mine_at] = gsend[side, pl.ds(pl.multiple_of(24 * mine_at, 8), 24), :]
+
+    ya_end(10)
+    xa_end(11)
+    for n in (6, 7, 8, 10):
+        xb_end(n)
+    to_columns(0)
+    yb_end(9)
+    yb_end(11)
+    to_columns(1)
 
     kx = lax.broadcasted_iota(jnp.int32, (NG, 128), 0)
     lane = lax.broadcasted_iota(jnp.int32, (NG, 128), 1)
@@ -477,9 +528,10 @@
         factors.append((256.0 / float(NG) ** 3) / jnp.sqrt(square))
     coulomb = jnp.concatenate(factors, axis=1)
 
-    wait_bytes(grecv.at[:15], gsem.at[1])
+    for side in range(2):
+        wait_bytes(grecv.at[side, :15], gsem.at[side])
     pencil = jnp.concatenate(
-        [grecv[:, 16 * unit : 16 * unit + 16, :].reshape(256, 128) for unit in range(3)], axis=1
+        [grecv[:, :, 8 * unit : 8 * unit + 8, :].reshape(256, 128) for unit in range(3)], axis=1
     )
     spectral = dot3_table_left(pair_of("forward_x"), pencil) * coulomb
     restored = dot3_table_left(pair_of("plain"), spectral)
@@ -540,7 +592,7 @@
     wait_bytes(yb_recv, sent.at[6])
     wait_bytes(precv.at[0, : 6 * PIECE], sent.at[7])
     wait_bytes(precv.at[0, : 8 * PIECE], sent.at[8])
-    wait_bytes(grecv.at[:15], gsem.at[0])
+    wait_bytes(grecv.at[:, :15], gsem.at[2])
     wait_bytes(wrecv.at[:21], wsem.at[0])
     wait_bytes(zrecv.at[:15], zsem.at[0])
 
@@ -566,19 +618,21 @@
             pltpu.VMEM((2, 4, ROWS, 128), F32),
             pltpu.VMEM((2, ROWS, 128), F32),
             pltpu.VMEM((2, 4 * ROWS, 128), F32),
-            pltpu.VMEM((8, 2, NG, NG), F32),
-            pltpu.VMEM((8, 2, NG, NG), F32),
-            pltpu.VMEM((8, 2, NG, NG), F32),
-            pltpu.VMEM((8, 3, 4, 2, 24, 128), F32),
-            pltpu.VMEM((4, 3, 3, 2, 24, 128), F32),
-            pltpu.VMEM((4, 3, 2, 24, 128), F32),
-            pltpu.VMEM((4, 3, 24, 128), F32),
-            pltpu.VMEM((4, 3, 4, 24, 128), F32),
-            pltpu.VMEM((4, 3, 4, 24, 128), F32),
-            pltpu.VMEM((4, 3, 3, 24, 128), F32),
-            pltpu.VMEM((8, 3, 24, 128), F32),
-            pltpu.VMEM((768, 128), F32),
-            pltpu.VMEM((16, 48, 128), F32),
+            pltpu.VMEM((8, NG, NG), F32),
+            pltpu.VMEM((8, NG, NG), F32),
+            pltpu.VMEM((12, 4, 64, NG), F32),
+            pltpu.VMEM((12, 4, 64, NG), F32),
+            pltpu.VMEM((12, 4, 64, NG), F32),
+            pltpu.VMEM((12, 2, 4, 2, 24, 128), F32),
+            pltpu.VMEM((10, 3, 2, 2, 24, 128), F32),
+            pltpu.VMEM((10, 2, 2, 24, 128), F32),
+            pltpu.VMEM((10, 2, 24, 128), F32),
+            pltpu.VMEM((2, 2, 4, 24, 128), F32),
+            pltpu.VMEM((2, 2, 4, 24, 128), F32),
+            pltpu.VMEM((2, 3, 2, 24, 128), F32),
+            pltpu.VMEM((3, 4, 2, 24, 128), F32),
+            pltpu.VMEM((2, 384, 128), F32),
+            pltpu.VMEM((2, 16, 24, 128), F32),
             pltpu.VMEM((3, NG, 128), F32),
             pltpu.VMEM((24, 24, 128), F32),
             pltpu.VMEM((2, 384, 128), F32),
@@ -586,15 +640,15 @@
             pltpu.VMEM((16, 16, 384), F32),
             pltpu.VMEM((384, 256), F32),
             dma((8,)),
-            dma((2, 2)),
+            dma((2, 3)),
             dma((2,)),
             dma((2,)),
-            dma((8,)),
-            dma((4,)),
-            dma((4,)),
-            dma((4,)),
-            dma((4,)),
+            dma((12,)),
+            dma((10,)),
+            dma((10,)),
             dma((2,)),
+            dma((2,)),
+            dma((3,)),
             dma((2,)),
             dma((2,)),
             dma((9,)),

time: 89.2 us -> 78.6 us (0.88)
  Pallas kernels: 85.9 us -> 75.2 us
    pallas_call x1, Pallas kernels: 85.9 us -> 75.2 us  [on_device(): pl.pallas_call(kernel, out_shape=jax.ShapeDtypeStruct((1, SLAB, 12, NG),...]
where the time goes in v3:
time: 78.6 us; the launch traced here: 78.4 us
  Pallas kernels  75.2 us (96%)
  local copies, waits for them, and re-layouts  1.88 us (2%)
  between operations  1.3 us (2%)
    pallas_call x1, Pallas kernels, on_device(): pl.pallas_call(kernel, out_shape=jax.ShapeDtypeStruct((1, SLAB, 12, NG),...  75.2 us
    pallas_call x1, local copies, waits for them, and re-layouts, on_device(): pl.pallas_call(kernel, out_shape=jax.ShapeDtypeStruct((1, SLAB, 12, NG),...  1.88 us

profile of v3, /device:TPU:1, one launch (start us, length us, event | category | flops | bytes accessed | tf_op | source)
XLA Modules:
  0.0 78.4 jit_solution(7416882704560368946)
XLA Ops:
  1.3 75.2 %response.1 = f32[1,24,12,192]{3,2,1,0:T(8,128)} custom-call(f32[1]{0:T(128)S(6)} %copy.8.occ_ref, f32[1]{0:T(128)S(6)} %copy.9.shift_ref, bf16[1,24,192,192]{3,2,1,0:T(8,128)(2,1)} %orb_hbm.1, f32[1,24,192,192]{3,2,1,0:T(8,128)} %pert_hbm.1, f32[24,192,192]{2,1,0:T(8,128)} %pot_hbm.1, bf16[3584,256]{1,0:T(8,128)(2,1)} %constant.2.clone.table_hbm), custom_call_target="tpu_custom_call" | custom-call | tf_op jit(solution)/shard_map/response/pallas_call | solution.py:605
  76.5 1.9 %copy.7 = f32[1,24,12,192]{3,1,2,0:T(8,128)} copy(f32[1,24,12,192]{3,2,1,0:T(8,128)} %response.1) | data formatting | bytes 442368 | tf_op jit(solution)/shard_map/response/pallas_call | solution.py:605

commit v4 on v3

--- a/solution.py
+++ b/solution.py
@@ -293,20 +293,26 @@
         e[layer + 8] = (a_own - b_own * diagonal) * value + b_sten * total
         return carry
 
-    def density_own(layer, chunk):
+    def fill_own(ref, n, base, chunk):
         rows = slice(64 * chunk, 64 * chunk + 64)
         around = {0: ((184, 192), (0, 72)), 1: ((56, 136),), 2: ((120, 192), (0, 8))}[chunk]
-        pieces = [e[layer + 4, lo:hi] for lo, hi in around]
-        high, low = split(pieces[0] if len(pieces) == 1 else jnp.concatenate(pieces, axis=0))
-        window = part("window")
-        total = along_x(e, layer + 4, rows) + (dot(window, high) + dot(window, low))
-        value = e[layer + 4, rows]
-        high, low = split(value)
-        stencil = part("stencil")
-        total += dot(high, stencil) + dot(low, stencil)
-        diagonal = pot[layer - 4, rows] + q_shift
-        solved = g0 * v[layer, rows] + (g1 - beta * diagonal) * value + beta_sten * total
-        return factor * orb[layer, rows].astype(F32) * solved
+        stencil, window = part("stencil"), part("window")
+        window = jnp.concatenate([window, window], axis=1)
+        high, low = split(e[pl.ds(base + 4, 4), rows].reshape(256, NG))
+        along_z = dot(high, stencil) + dot(low, stencil)
+        for i in range(4):
+            layer = base + i
+            pieces = [e[layer + 4, lo:hi] for lo, hi in around]
+            pieces = pieces[0] if len(pieces) == 1 else jnp.concatenate(pieces, axis=0)
+            along_y = dot(window, jnp.concatenate(split(pieces), axis=0))
+            total = along_x(e, layer + 4, rows) + (along_y + along_z[64 * i : 64 * i + 64])
+            diagonal = pot[layer - 4, rows] + q_shift
+            solved = (
+                g0 * v[layer, rows]
+                + (g1 - beta * diagonal) * e[layer + 4, rows]
+                + beta_sten * total
+            )
+            ref[n, i] = factor * orb[layer, rows].astype(F32) * solved
 
     def density_beyond(layer, chunk):
         rows = slice(64 * chunk, 64 * chunk + 64)
@@ -315,13 +321,15 @@
 
     def make_item(n):
         chunk, block = ITEMS[n]
-        density = density_beyond if block == 3 else density_own
 
         def fill(ref, c):
             base = jnp.where(c == 0, 12 - 4 * block, 16 + 4 * block)
+            if block < 3:
+                fill_own(ref, n, base, chunk)
+                return
 
             def body(layer, carry):
-                ref[n, layer] = density(base + layer, chunk)
+                ref[n, layer] = density_beyond(base + layer, chunk)
                 return carry
 
             lax.fori_loop(0, 4, body, 0)
@@ -391,7 +399,7 @@
         wait_bytes(yb_recv.at[i], yb_sem.at[i])
         red[chunk, block] = (ysum[i, :, y] + yb_recv[i, 0]) + (yb_recv[i, 1] + yb_recv[i, 2])
 
-    lax.fori_loop(4, 12, make_e, 0)
+    lax.fori_loop(4, 20, make_e, 0)
 
     for way in range(2):
         wait_bytes(precv.at[way, :PIECE], psem.at[way])
@@ -402,8 +410,11 @@
                 precv.at[way, pl.ds(piece_row, PIECE)],
                 sent.at[7], fsem.at[0], band_of(x_lo, y_at(k), core), space,
             )
-    lax.fori_loop(12, 20, make_e, 0)
     make_item(0)
+    make_item(1)
+    make_item(2)
+    lax.fori_loop(0, 4, make_e, 0)
+    lax.fori_loop(20, 24, make_e, 0)
     wait_bytes(precv.at[0, : 6 * PIECE], fsem.at[0])
     core_row = pl.multiple_of(core * 4 * PIECE, 8)
     for way in range(2):
@@ -412,13 +423,9 @@
             precv.at[way, pl.ds(core_row, 4 * PIECE)],
             sent.at[8], fsem.at[1], band_of(x_lo, y, 1 - core), space,
         )
-    make_item(1)
     ya_start(0)
-    make_item(2)
     ya_start(1)
-    lax.fori_loop(0, 4, make_e, 0)
     ya_start(2)
-    lax.fori_loop(20, 24, make_e, 0)
 
     def take_halo(chunk):
         start, count, places = CHUNKS[chunk]
@@ -538,35 +545,39 @@
     for unit in range(3):
         wsend[unit] = restored[:, 128 * unit : 128 * unit + 128]
 
-    for k in (4, 3, 5, 2, 6, 1, 7):
-        to_space = lax.rem(space + k, 8)
-        row = pl.multiple_of(24 * to_space, 8)
-        send(
-            wsend.at[:, pl.ds(row, 24)], wrecv.at[pl.ds(3 * space, 3)],
-            wsem.at[0], wsem.at[1], band, to_space,
-        )
-    wrecv[pl.ds(3 * space, 3)] = wsend[:, pl.ds(pl.multiple_of(24 * space, 8), 24), :]
+    for third in range(3):
+        for k in (4, 3, 5, 2, 6, 1, 7):
+            to_space = lax.rem(space + k, 8)
+            row = pl.multiple_of(24 * to_space + 8 * third, 8)
+            send(
+                wsend.at[:, pl.ds(row, 8)], wrecv.at[third, pl.ds(3 * space, 3)],
+                wsem.at[3], wsem.at[third], band, to_space,
+            )
+    for third in range(3):
+        own_row = pl.multiple_of(24 * space + 8 * third, 8)
+        wrecv[third, pl.ds(3 * space, 3)] = wsend[:, pl.ds(own_row, 8), :]
     brow[...] = jnp.zeros(brow.shape, F32)
-    wait_bytes(wrecv.at[:21], wsem.at[1])
-
-    for unit in range(24):
-        brow[unit % 2, pl.ds(unit // 2, 24, stride=16), :] = wrecv[unit]
-    rows = jnp.concatenate([brow[0], brow[1]], axis=1)
-    zsend[...] = dot3_table_left(pair_of("inverse_y"), rows, ((1,), (1,)))
-
-    for k in (4, 12, 8, 3, 5, 11, 13, 2, 6, 10, 14, 7, 9, 1, 15):
-        to = lax.rem(band + k, 16)
-        send(
-            zsend.at[pl.ds(pl.multiple_of(16 * to, 8), 16)], zrecv.at[band],
-            zsem.at[0], zsem.at[1], to, space,
-        )
-    zrecv[band] = zsend[pl.ds(pl.multiple_of(16 * band, 8), 16), :]
-    wait_bytes(zrecv.at[:15], zsem.at[1])
+    for third in range(3):
+        wait_bytes(wrecv.at[third, :21], wsem.at[third])
+        for unit in range(24):
+            brow[unit % 2, pl.ds(128 * third + unit // 2, 8, stride=16), :] = wrecv[third, unit]
+        rows = jnp.concatenate(
+            [brow[half, 128 * third : 128 * third + 128] for half in range(2)], axis=1
+        )
+        zsend[third] = dot3_table_left(pair_of("inverse_y"), rows, ((1,), (1,)))
+        for k in (4, 12, 8, 3, 5, 11, 13, 2, 6, 10, 14, 7, 9, 1, 15):
+            to = lax.rem(band + k, 16)
+            send(
+                zsend.at[third, pl.ds(pl.multiple_of(16 * to, 8), 16)], zrecv.at[third, band],
+                zsem.at[3], zsem.at[third], to, space,
+            )
+        zrecv[third, band] = zsend[third, pl.ds(pl.multiple_of(16 * band, 8), 16), :]
 
     granule = lax.broadcasted_iota(jnp.int32, (16, 128), 1) // 16
     for third in range(3):
+        wait_bytes(zrecv.at[third, :15], zsem.at[third])
         for side in range(2):
-            blocks = [zrecv[8 * side + i, :, 128 * third : 128 * third + 128] for i in range(8)]
+            blocks = [zrecv[third, 8 * side + i] for i in range(8)]
             for bit in (1, 2, 4):
                 upper = lax.rem(granule // bit, 2) == 1
                 after = list(blocks)
@@ -577,11 +588,10 @@
                         after[i | bit] = jnp.where(upper, high, pltpu.roll(low, 128 - 16 * bit, 1))
                 blocks = after
             for i in range(8):
-                x = 8 * third + i
-                mat[16 * x : 16 * x + 16, 128 * side : 128 * side + 128] = blocks[i]
-    result = dot3_table_right(mat[...], pair_of("inverse_z"))
-    for x in range(SLAB):
-        out[0, x] = result[16 * x : 16 * x + 12]
+                mat[side, pl.ds(i, 16, stride=8), :] = blocks[i]
+        rows = jnp.concatenate([mat[0, :96], mat[1, :96]], axis=1)
+        result = dot3_table_right(rows, pair_of("inverse_z"))
+        out[0, :, 8 * third : 8 * third + 8] = result.reshape(12, 8, NG)
 
     wait_bytes(psend.at[:, :PIECE], sent.at[0])
     wait_bytes(osend, sent.at[1])
@@ -593,8 +603,8 @@
     wait_bytes(precv.at[0, : 6 * PIECE], sent.at[7])
     wait_bytes(precv.at[0, : 8 * PIECE], sent.at[8])
     wait_bytes(grecv.at[:, :15], gsem.at[2])
-    wait_bytes(wrecv.at[:21], wsem.at[0])
-    wait_bytes(zrecv.at[:15], zsem.at[0])
+    wait_bytes(wrecv.at[:, :21], wsem.at[3])
+    wait_bytes(zrecv.at[:, :15], zsem.at[3])
 
 
 def on_device(orbitals, occupations, shifts, perturbations, local_potential):
@@ -602,9 +612,9 @@
     smem = pl.BlockSpec(memory_space=pltpu.SMEM)
     vmem = pl.BlockSpec(memory_space=pltpu.VMEM)
     dma = pltpu.SemaphoreType.DMA
-    return pl.pallas_call(
+    response = pl.pallas_call(
         kernel,
-        out_shape=jax.ShapeDtypeStruct((1, SLAB, 12, NG), F32),
+        out_shape=jax.ShapeDtypeStruct((1, 12, SLAB, NG), F32),
         in_specs=[smem] * 2 + [any_space] * 4,
         out_specs=vmem,
         scratch_shapes=[
@@ -634,11 +644,11 @@
             pltpu.VMEM((2, 384, 128), F32),
             pltpu.VMEM((2, 16, 24, 128), F32),
             pltpu.VMEM((3, NG, 128), F32),
-            pltpu.VMEM((24, 24, 128), F32),
+            pltpu.VMEM((3, 24, 8, 128), F32),
             pltpu.VMEM((2, 384, 128), F32),
-            pltpu.VMEM((256, 384), F32),
-            pltpu.VMEM((16, 16, 384), F32),
-            pltpu.VMEM((384, 256), F32),
+            pltpu.VMEM((3, 256, 128), F32),
+            pltpu.VMEM((3, 16, 16, 128), F32),
+            pltpu.VMEM((2, 128, 128), F32),
             dma((8,)),
             dma((2, 3)),
             dma((2,)),
@@ -649,8 +659,8 @@
             dma((2,)),
             dma((2,)),
             dma((3,)),
-            dma((2,)),
-            dma((2,)),
+            dma((4,)),
+            dma((4,)),
             dma((9,)),
         ],
         compiler_params=pltpu.CompilerParams(
@@ -658,6 +668,7 @@
         ),
         name="response",
     )(occupations, shifts, orbitals, perturbations, local_potential, jnp.asarray(TABLE))
+    return jnp.transpose(response, (0, 2, 1, 3))
 
 
 def solution(mesh):

time: 78.6 us -> 75.5 us (0.961)
  Pallas kernels: 75.2 us -> 72.4 us
    pallas_call x1, Pallas kernels: 75.2 us -> 72.4 us  [on_device(): pl.pallas_call(kernel, out_shape=jax.ShapeDtypeStruct((1, 12, SLAB, NG),...]
    pallas_call x1 -> x0, local copies, waits for them, and re-layouts: 1.88 us -> none  [on_device(): pl.pallas_call(kernel, out_shape=jax.ShapeDtypeStruct((1, SLAB, 12, NG),...]
    unnamed x0 -> x1, local copies, waits for them, and re-layouts: none -> 1.69 us
where the time goes in v4:
time: 75.5 us; the launch traced here: 75.4 us
  Pallas kernels  72.4 us (96%)
  local copies, waits for them, and re-layouts  1.69 us (2%)
  between operations  1.31 us (2%)
    pallas_call x1, Pallas kernels, on_device(): pl.pallas_call(kernel, out_shape=jax.ShapeDtypeStruct((1, 12, SLAB, NG),...  72.4 us
    unnamed x1, local copies, waits for them, and re-layouts  1.69 us

profile of v4, /device:TPU:1, one launch (start us, length us, event | category | flops | bytes accessed | tf_op | source)
XLA Modules:
  0.0 75.4 jit_solution(1190644133833846628)
XLA Ops:
  1.3 72.4 %response.1 = f32[1,12,24,192]{3,2,1,0:T(8,128)} custom-call(f32[1]{0:T(128)S(6)} %copy.8.occ_ref, f32[1]{0:T(128)S(6)} %copy.9.shift_ref, bf16[1,24,192,192]{3,2,1,0:T(8,128)(2,1)} %orb_hbm.1, f32[1,24,192,192]{3,2,1,0:T(8,128)} %pert_hbm.1, f32[24,192,192]{2,1,0:T(8,128)} %pot_hbm.1, bf16[3584,256]{1,0:T(8,128)(2,1)} %constant.2.clone.table_hbm), custom_call_target="tpu_custom_call" | custom-call | tf_op jit(solution)/shard_map/response/pallas_call | solution.py:615
  73.7 1.7 %copy.10 = f32[1,24,12,192]{3,1,2,0:T(8,128)} copy(f32[1,24,12,192]{3,1,2,0:T(8,128)} %bitcast.1) | data formatting | bytes 442368

commit v5 on v4

--- a/solution.py
+++ b/solution.py
@@ -65,10 +65,10 @@
                 x = (SLAB * space + ext - 4) % NG
                 column = 128 * (slot // 8) + (core * 8 + space) * 8 + slot % 8
                 forward_x[:, column] = plain[:, x]
-    inverse_y = np.zeros((256, 256))
+    inverse_y = np.zeros((NG, 256))
+    inverse_y[:, :NG] = plain
     inverse_z = np.zeros((256, NG))
     for band in range(16):
-        inverse_y[band * 16 : band * 16 + 12, :NG] = plain[band * 12 : band * 12 + 12]
         x_lo, y, core = band // 8, (band // 2) % 4, band % 2
         first = 24 * (2 * y + x_lo) + 12 * core
         inverse_z[band * 16 : band * 16 + 12] = plain[first : first + 12]
@@ -143,7 +143,7 @@
     table, orb, pert, pot, v, e,
     osend, orecv, psend, precv, orb_halo, v_halo,
     mine, other, crecv, tiles, ya_recv, xsum, xb_recv, xa_recv, ysum, yb_recv, red,
-    gsend, grecv, wsend, wrecv, brow, zsend, zrecv, mat,
+    ready, gsend, grecv, wsend, wrecv, brow, zsend, zrecv, mat,
     load_sem, osem, psem, fsem, csem, ya_sem, xb_sem, xa_sem, yb_sem, gsem, wsem, zsem, sent,
 ):
     band = lax.axis_index("band")
@@ -293,19 +293,26 @@
         e[layer + 8] = (a_own - b_own * diagonal) * value + b_sten * total
         return carry
 
-    def fill_own(ref, n, base, chunk):
+    def in_plane(base, chunk):
         rows = slice(64 * chunk, 64 * chunk + 64)
         around = {0: ((184, 192), (0, 72)), 1: ((56, 136),), 2: ((120, 192), (0, 8))}[chunk]
         stencil, window = part("stencil"), part("window")
         window = jnp.concatenate([window, window], axis=1)
         high, low = split(e[pl.ds(base + 4, 4), rows].reshape(256, NG))
         along_z = dot(high, stencil) + dot(low, stencil)
+        totals = []
+        for i in range(4):
+            pieces = [e[base + i + 4, lo:hi] for lo, hi in around]
+            pieces = pieces[0] if len(pieces) == 1 else jnp.concatenate(pieces, axis=0)
+            along_y = dot(window, jnp.concatenate(split(pieces), axis=0))
+            totals.append(along_y + along_z[64 * i : 64 * i + 64])
+        return totals
+
+    def fill_own(ref, n, base, chunk, totals):
+        rows = slice(64 * chunk, 64 * chunk + 64)
         for i in range(4):
             layer = base + i
-            pieces = [e[layer + 4, lo:hi] for lo, hi in around]
-            pieces = pieces[0] if len(pieces) == 1 else jnp.concatenate(pieces, axis=0)
-            along_y = dot(window, jnp.concatenate(split(pieces), axis=0))
-            total = along_x(e, layer + 4, rows) + (along_y + along_z[64 * i : 64 * i + 64])
+            total = along_x(e, layer + 4, rows) + totals[i]
             diagonal = pot[layer - 4, rows] + q_shift
             solved = (
                 g0 * v[layer, rows]
@@ -314,6 +321,15 @@
             )
             ref[n, i] = factor * orb[layer, rows].astype(F32) * solved
 
+    def base_of(c, block):
+        return jnp.where(c == 0, 12 - 4 * block, 16 + 4 * block)
+
+    def prepare(n):
+        chunk, block = ITEMS[n]
+        for which, c in ((0, 1 - core), (1, core)):
+            for i, total in enumerate(in_plane(base_of(c, block), chunk)):
+                ready[which, i] = total
+
     def density_beyond(layer, chunk):
         rows = slice(64 * chunk, 64 * chunk + 64)
         at = jnp.where(layer < 4, layer, layer - 24)
@@ -323,9 +339,14 @@
         chunk, block = ITEMS[n]
 
         def fill(ref, c):
-            base = jnp.where(c == 0, 12 - 4 * block, 16 + 4 * block)
+            base = base_of(c, block)
             if block < 3:
-                fill_own(ref, n, base, chunk)
+                if n == 10:
+                    which = 0 if ref is other else 1
+                    totals = [ready[which, i] for i in range(4)]
+                else:
+                    totals = in_plane(base, chunk)
+                fill_own(ref, n, base, chunk, totals)
                 return
 
             def body(layer, carry):
@@ -469,6 +490,7 @@
     make_item(8)
     ya_start(7)
     ya_start(8)
+    prepare(10)
     for n in range(3, 6):
         ya_end(n)
     take_halo(2)
@@ -500,7 +522,7 @@
                     gsend[side, pl.ds(half * 8 + 2 * j + layer, 24, stride=16), :] = columns[
                         24 * j : 24 * j + 24, 128 * half : 128 * half + 128
                     ]
-        for k in (4, 3, 5, 2, 6, 1, 7, 0):
+        for k in (3, 5, 1, 7, 4, 2, 6, 0):
             for c in range(2):
                 if (k, c) != (0, 0):
                     to_space = lax.rem(space + k, 8)
@@ -546,7 +568,7 @@
         wsend[unit] = restored[:, 128 * unit : 128 * unit + 128]
 
     for third in range(3):
-        for k in (4, 3, 5, 2, 6, 1, 7):
+        for k in (3, 5, 1, 7, 4, 2, 6):
             to_space = lax.rem(space + k, 8)
             row = pl.multiple_of(24 * to_space + 8 * third, 8)
             send(
@@ -564,20 +586,20 @@
         rows = jnp.concatenate(
             [brow[half, 128 * third : 128 * third + 128] for half in range(2)], axis=1
         )
-        zsend[third] = dot3_table_left(pair_of("inverse_y"), rows, ((1,), (1,)))
+        zsend[third] = dot3_table_left(pair_of("inverse_y"), rows, ((1,), (1,))).reshape(48, 4, 128)
         for k in (4, 12, 8, 3, 5, 11, 13, 2, 6, 10, 14, 7, 9, 1, 15):
             to = lax.rem(band + k, 16)
             send(
-                zsend.at[third, pl.ds(pl.multiple_of(16 * to, 8), 16)], zrecv.at[third, band],
+                zsend.at[third, pl.ds(3 * to, 3)], zrecv.at[third, band],
                 zsem.at[3], zsem.at[third], to, space,
             )
-        zrecv[third, band] = zsend[third, pl.ds(pl.multiple_of(16 * band, 8), 16), :]
-
-    granule = lax.broadcasted_iota(jnp.int32, (16, 128), 1) // 16
+        zrecv[third, band] = zsend[third, pl.ds(3 * band, 3)]
+
+    granule = lax.broadcasted_iota(jnp.int32, (12, 128), 1) // 16
     for third in range(3):
         wait_bytes(zrecv.at[third, :15], zsem.at[third])
         for side in range(2):
-            blocks = [zrecv[third, 8 * side + i] for i in range(8)]
+            blocks = [zrecv[third, 8 * side + i].reshape(12, 128) for i in range(8)]
             for bit in (1, 2, 4):
                 upper = lax.rem(granule // bit, 2) == 1
                 after = list(blocks)
@@ -588,8 +610,8 @@
                         after[i | bit] = jnp.where(upper, high, pltpu.roll(low, 128 - 16 * bit, 1))
                 blocks = after
             for i in range(8):
-                mat[side, pl.ds(i, 16, stride=8), :] = blocks[i]
-        rows = jnp.concatenate([mat[0, :96], mat[1, :96]], axis=1)
+                mat[side, pl.ds(i, 12, stride=8), :] = blocks[i]
+        rows = jnp.concatenate([mat[0], mat[1]], axis=1)
         result = dot3_table_right(rows, pair_of("inverse_z"))
         out[0, :, 8 * third : 8 * third + 8] = result.reshape(12, 8, NG)
 
@@ -641,14 +663,15 @@
             pltpu.VMEM((2, 2, 4, 24, 128), F32),
             pltpu.VMEM((2, 3, 2, 24, 128), F32),
             pltpu.VMEM((3, 4, 2, 24, 128), F32),
+            pltpu.VMEM((2, 4, 64, NG), F32),
             pltpu.VMEM((2, 384, 128), F32),
             pltpu.VMEM((2, 16, 24, 128), F32),
             pltpu.VMEM((3, NG, 128), F32),
             pltpu.VMEM((3, 24, 8, 128), F32),
             pltpu.VMEM((2, 384, 128), F32),
-            pltpu.VMEM((3, 256, 128), F32),
-            pltpu.VMEM((3, 16, 16, 128), F32),
-            pltpu.VMEM((2, 128, 128), F32),
+            pltpu.VMEM((3, 48, 4, 128), F32),
+            pltpu.VMEM((3, 16, 3, 4, 128), F32),
+            pltpu.VMEM((2, 96, 128), F32),
             dma((8,)),
             dma((2, 3)),
             dma((2,)),

time: 75.5 us -> 74.7 us (0.989)
  Pallas kernels: 72.4 us -> 71.6 us
    pallas_call x1, Pallas kernels: 72.4 us -> 71.6 us  [on_device(): pl.pallas_call(kernel, out_shape=jax.ShapeDtypeStruct((1, 12, SLAB, NG),...]
where the time goes in v5:
time: 74.7 us; the launch traced here: 74.6 us
  Pallas kernels  71.6 us (96%)
  local copies, waits for them, and re-layouts  1.69 us (2%)
  between operations  1.31 us (2%)
    pallas_call x1, Pallas kernels, on_device(): pl.pallas_call(kernel, out_shape=jax.ShapeDtypeStruct((1, 12, SLAB, NG),...  71.6 us
    unnamed x1, local copies, waits for them, and re-layouts  1.69 us

profile of v5, /device:TPU:1, one launch (start us, length us, event | category | flops | bytes accessed | tf_op | source)
XLA Modules:
  0.0 74.6 jit_solution(3156628208127187789)
XLA Ops:
  1.3 71.6 %response.1 = f32[1,12,24,192]{3,2,1,0:T(8,128)} custom-call(f32[1]{0:T(128)S(6)} %copy.8.occ_ref, f32[1]{0:T(128)S(6)} %copy.9.shift_ref, bf16[1,24,192,192]{3,2,1,0:T(8,128)(2,1)} %orb_hbm.1, f32[1,24,192,192]{3,2,1,0:T(8,128)} %pert_hbm.1, f32[24,192,192]{2,1,0:T(8,128)} %pot_hbm.1, bf16[3456,256]{1,0:T(8,128)(2,1)} %constant.2.clone.table_hbm), custom_call_target="tpu_custom_call" | custom-call | tf_op jit(solution)/shard_map/response/pallas_call | solution.py:637
  72.9 1.7 %copy.10 = f32[1,24,12,192]{3,1,2,0:T(8,128)} copy(f32[1,24,12,192]{3,1,2,0:T(8,128)} %bitcast.1) | data formatting | bytes 442368

commit v6 on v5

--- a/solution.py
+++ b/solution.py
@@ -25,7 +25,7 @@
 )
 ITEMS = ((0, 0), (1, 0), (2, 0), (0, 1), (0, 2), (0, 3), (1, 1), (1, 2), (1, 3), (2, 3), (2, 1), (2, 2))
 X_FIRST = (9, 11)
-Y_FIRST = tuple(n for n in range(12) if n not in X_FIRST)
+Y_FIRST = tuple(range(9))
 
 
 def cas(product):
@@ -142,9 +142,9 @@
     occ_ref, shift_ref, orb_hbm, pert_hbm, pot_hbm, table_hbm, out,
     table, orb, pert, pot, v, e,
     osend, orecv, psend, precv, orb_halo, v_halo,
-    mine, other, crecv, tiles, ya_recv, xsum, xb_recv, xa_recv, ysum, yb_recv, red,
+    mine, other, crecv, tiles, ya_recv, xsum, xb_recv, xa_recv, ysum, yb_recv, d_recv, red,
     ready, gsend, grecv, wsend, wrecv, brow, zsend, zrecv, mat,
-    load_sem, osem, psem, fsem, csem, ya_sem, xb_sem, xa_sem, yb_sem, gsem, wsem, zsem, sent,
+    load_sem, osem, psem, fsem, csem, ya_sem, xb_sem, xa_sem, yb_sem, d_sem, gsem, wsem, zsem, sent,
 ):
     band = lax.axis_index("band")
     space = lax.axis_index("space")
@@ -419,6 +419,24 @@
         chunk, block = ITEMS[n]
         wait_bytes(yb_recv.at[i], yb_sem.at[i])
         red[chunk, block] = (ysum[i, :, y] + yb_recv[i, 0]) + (yb_recv[i, 1] + yb_recv[i, 2])
+
+    def d_start(n):
+        add_cores(n)
+        for k in (6, 2, 5, 7, 1, 3, 4):
+            x_to = x_lo if k < 4 else 1 - x_lo
+            y_to = y_at(k % 4)
+            send(
+                tiles.at[n, :, y_to, x_to], d_recv.at[k - 1],
+                d_sem.at[0], d_sem.at[1], band_of(x_to, y_to, core), space,
+            )
+
+    def d_end(n):
+        chunk, block = ITEMS[n]
+        wait_bytes(d_recv, d_sem.at[1])
+        total = tiles[n, :, y, x_lo] + d_recv[0]
+        for k in range(1, 7):
+            total += d_recv[k]
+        red[chunk, block] = total
 
     lax.fori_loop(4, 20, make_e, 0)
 
@@ -498,7 +516,7 @@
     make_item(10)
     xa_start(9)
     make_item(11)
-    ya_start(10)
+    d_start(10)
     xa_start(11)
     for n in range(6, 9):
         ya_end(n)
@@ -534,11 +552,12 @@
                     )
         grecv[side, mine_at] = gsend[side, pl.ds(pl.multiple_of(24 * mine_at, 8), 24), :]
 
-    ya_end(10)
+    xb_end(6)
+    d_end(10)
     xa_end(11)
-    for n in (6, 7, 8, 10):
-        xb_end(n)
     to_columns(0)
+    xb_end(7)
+    xb_end(8)
     yb_end(9)
     yb_end(11)
     to_columns(1)
@@ -622,6 +641,7 @@
     wait_bytes(xb_recv, sent.at[4])
     wait_bytes(xa_recv, sent.at[5])
     wait_bytes(yb_recv, sent.at[6])
+    wait_bytes(d_recv, d_sem.at[0])
     wait_bytes(precv.at[0, : 6 * PIECE], sent.at[7])
     wait_bytes(precv.at[0, : 8 * PIECE], sent.at[8])
     wait_bytes(grecv.at[:, :15], gsem.at[2])
@@ -656,12 +676,13 @@
             pltpu.VMEM((12, 4, 64, NG), F32),
             pltpu.VMEM((12, 4, 64, NG), F32),
             pltpu.VMEM((12, 2, 4, 2, 24, 128), F32),
-            pltpu.VMEM((10, 3, 2, 2, 24, 128), F32),
-            pltpu.VMEM((10, 2, 2, 24, 128), F32),
-            pltpu.VMEM((10, 2, 24, 128), F32),
+            pltpu.VMEM((9, 3, 2, 2, 24, 128), F32),
+            pltpu.VMEM((9, 2, 2, 24, 128), F32),
+            pltpu.VMEM((9, 2, 24, 128), F32),
             pltpu.VMEM((2, 2, 4, 24, 128), F32),
             pltpu.VMEM((2, 2, 4, 24, 128), F32),
             pltpu.VMEM((2, 3, 2, 24, 128), F32),
+            pltpu.VMEM((7, 2, 24, 128), F32),
             pltpu.VMEM((3, 4, 2, 24, 128), F32),
             pltpu.VMEM((2, 4, 64, NG), F32),
             pltpu.VMEM((2, 384, 128), F32),
@@ -677,8 +698,9 @@
             dma((2,)),
             dma((2,)),
             dma((12,)),
-            dma((10,)),
-            dma((10,)),
+            dma((9,)),
+            dma((9,)),
+            dma((2,)),
             dma((2,)),
             dma((2,)),
             dma((3,)),

time: 74.7 us -> 76.8 us (1.028)
  Pallas kernels: 71.6 us -> 73.7 us
    pallas_call x1, Pallas kernels: 71.6 us -> 73.7 us  [on_device(): pl.pallas_call(kernel, out_shape=jax.ShapeDtypeStruct((1, 12, SLAB, NG),...]
where the time goes in v6:
time: 76.8 us; the launch traced here: 76.7 us
  Pallas kernels  73.7 us (96%)
  local copies, waits for them, and re-layouts  1.69 us (2%)
  between operations  1.31 us (2%)
    pallas_call x1, Pallas kernels, on_device(): pl.pallas_call(kernel, out_shape=jax.ShapeDtypeStruct((1, 12, SLAB, NG),...  73.7 us
    unnamed x1, local copies, waits for them, and re-layouts  1.69 us

profile of v6, /device:TPU:1, one launch (start us, length us, event | category | flops | bytes accessed | tf_op | source)
XLA Modules:
  0.0 76.7 jit_solution(15958894240488154669)
XLA Ops:
  1.3 73.7 %response.1 = f32[1,12,24,192]{3,2,1,0:T(8,128)} custom-call(f32[1]{0:T(128)S(6)} %copy.8.occ_ref, f32[1]{0:T(128)S(6)} %copy.9.shift_ref, bf16[1,24,192,192]{3,2,1,0:T(8,128)(2,1)} %orb_hbm.1, f32[1,24,192,192]{3,2,1,0:T(8,128)} %pert_hbm.1, f32[24,192,192]{2,1,0:T(8,128)} %pot_hbm.1, bf16[3456,256]{1,0:T(8,128)(2,1)} %constant.2.clone.table_hbm), custom_call_target="tpu_custom_call" | custom-call | tf_op jit(solution)/shard_map/response/pallas_call | solution.py:657
  75.0 1.7 %copy.10 = f32[1,24,12,192]{3,1,2,0:T(8,128)} copy(f32[1,24,12,192]{3,1,2,0:T(8,128)} %bitcast.1) | data formatting | bytes 442368

commit v7 on v5

--- a/solution.py
+++ b/solution.py
@@ -495,11 +495,11 @@
         ya_end(n)
     take_halo(2)
     make_item(9)
+    make_item(11)
+    xa_start(9)
     make_item(10)
-    xa_start(9)
-    make_item(11)
+    xa_start(11)
     ya_start(10)
-    xa_start(11)
     for n in range(6, 9):
         ya_end(n)
     xa_end(9)

time: 74.7 us -> 75.4 us (level)
  no operation moved by 1% of the time
where the time goes in v7:
time: 75.4 us; the launch traced here: 75.3 us
  Pallas kernels  72.3 us (96%)
  local copies, waits for them, and re-layouts  1.69 us (2%)
  between operations  1.31 us (2%)
    pallas_call x1, Pallas kernels, on_device(): pl.pallas_call(kernel, out_shape=jax.ShapeDtypeStruct((1, 12, SLAB, NG),...  72.3 us
    unnamed x1, local copies, waits for them, and re-layouts  1.69 us

profile of v7, /device:TPU:1, one launch (start us, length us, event | category | flops | bytes accessed | tf_op | source)
XLA Modules:
  0.0 75.3 jit_solution(4777276868369704717)
XLA Ops:
  1.3 72.3 %response.1 = f32[1,12,24,192]{3,2,1,0:T(8,128)} custom-call(f32[1]{0:T(128)S(6)} %copy.8.occ_ref, f32[1]{0:T(128)S(6)} %copy.9.shift_ref, bf16[1,24,192,192]{3,2,1,0:T(8,128)(2,1)} %orb_hbm.1, f32[1,24,192,192]{3,2,1,0:T(8,128)} %pert_hbm.1, f32[24,192,192]{2,1,0:T(8,128)} %pot_hbm.1, bf16[3456,256]{1,0:T(8,128)(2,1)} %constant.2.clone.table_hbm), custom_call_target="tpu_custom_call" | custom-call | tf_op jit(solution)/shard_map/response/pallas_call | solution.py:637
  73.6 1.7 %copy.10 = f32[1,24,12,192]{3,1,2,0:T(8,128)} copy(f32[1,24,12,192]{3,1,2,0:T(8,128)} %bitcast.1) | data formatting | bytes 442368
